TPU v7x, 32 devices: a whole 2x2x4 slice. The times are simulated.
32 devices in a mesh: grp: 4 (over x, core), ep: 8 (over z, y).
Axes of the slice: x: 2, y: 2, z: 4, core: 2. Of those that a mesh axis runs over, the one named last changes fastest.
Arguments:
- tokens_in: bfloat16 [4096, 2048], P(('grp', 'ep')), may hold values from -6 to 6
- grad_out: bfloat16 [4096, 2048], P(('grp', 'ep')), may hold values from -6 to 6
- replica_of: int32 [4096, 2], P(('grp', 'ep')), may hold values from 0 to 31, all different within a row; in each aligned block of 128 rows (0 to 127, 128 to 255, ...) at most 16 rows name the same one
- gate_weights: bfloat16 [4096, 2], P(('grp', 'ep')), may hold values from 0.099609375 to 1
- placement: int32 [4, 8], replicated, may hold values from 0 to 1, as said below
- w_in_rep: bfloat16 [4, 8, 2048, 1024], P('grp', 'ep'), as said below
- w_down_rep: bfloat16 [4, 8, 2048, 512], P('grp', 'ep'), as said below
Outputs:
- d_tokens: bfloat16 [4096, 2048], P(('grp', 'ep'))
- d_gates: bfloat16 [4096, 2], P(('grp', 'ep'))
- grad_in: bfloat16 [16, 2048, 1024], P('ep', 'grp')
- grad_down: bfloat16 [16, 2048, 512], P('ep', 'grp')
Inputs may be any that keep to these rules, and one draw needn't show every extreme that they name: `replica_of`: A row names a replica device by its index in the order grp then ep. The 2 rows of a token name different devices. At most 16 of the rows of one device name the same replica device, and some device sends exactly 16 rows to one replica. placement[g, e] selects expert e * 2 + placement[g, e]; in every column e each of the 2 values occurs at least once, so every expert has at least one copy. w_in_rep[g, e] and w_in_rep[g2, e] are equal wherever placement[g, e] equals placement[g2, e]. w_down_rep[g, e] and w_down_rep[g2, e] are equal wherever placement[g, e] equals placement[g2, e].
All inputs are finite; a program needn't handle non-finite values.
Results may differ from a plain program's by a relative error of at most 0.01.
Values may be sent and summed in bfloat16 or wider, within the bound.
A program may use at most 128 MiB of HBM per device.

v0:
```python
import jax
import jax.numpy as jnp
from jax import lax
from jax.sharding import PartitionSpec as P

KPC = 2


def expert_backward(rows_x, rows_dy, rows_gate, w_in, w_down):
    hidden = w_down.shape[1]
    both = jnp.dot(rows_x, w_in, preferred_element_type=jnp.float32)
    gate_pre = both[:, :hidden]
    up_part = both[:, hidden:]
    sigmoid_gate = jax.nn.sigmoid(gate_pre)
    silu_gate = gate_pre * sigmoid_gate
    activation = (silu_gate * up_part).astype(jnp.bfloat16)
    out_rows = lax.dot_general(
        activation, w_down, (((1,), (1,)), ((), ())), preferred_element_type=jnp.float32
    )
    gate_grad = jnp.sum(rows_dy.astype(jnp.float32) * out_rows, axis=1).astype(jnp.bfloat16)
    out_grad = (rows_gate.astype(jnp.float32)[:, None] * rows_dy.astype(jnp.float32)).astype(
        jnp.bfloat16
    )
    act_grad = jnp.dot(out_grad, w_down, preferred_element_type=jnp.float32)
    gate_grad_pre = act_grad * up_part * sigmoid_gate * (1.0 + gate_pre * (1.0 - sigmoid_gate))
    up_grad = act_grad * silu_gate
    both_grad = jnp.concatenate([gate_grad_pre, up_grad], axis=1).astype(jnp.bfloat16)
    row_grad = lax.dot_general(
        both_grad, w_in, (((1,), (1,)), ((), ())), preferred_element_type=jnp.float32
    ).astype(jnp.bfloat16)
    part_in = lax.dot_general(
        rows_x, both_grad, (((0,), (0,)), ((), ())), preferred_element_type=jnp.float32
    )
    part_down = lax.dot_general(
        out_grad, activation, (((0,), (0,)), ((), ())), preferred_element_type=jnp.float32
    )
    return (row_grad, gate_grad, part_in, part_down)


def shards(tokens_in, grad_out, replica_of, gate_weights, placement, w_in_rep, w_down_rep):
    tok_count, model_width = tokens_in.shape
    top_count = replica_of.shape[1]
    group_count = lax.axis_size("grp")
    lane_count = lax.axis_size("ep")
    device_count = group_count * lane_count
    capacity = max(2, 2 * tok_count * top_count // device_count)
    w_in = w_in_rep[0, 0]
    w_down = w_down_rep[0, 0]
    dest_rows = replica_of.reshape(-1)
    row_count = tok_count * top_count
    row_ids = jnp.arange(row_count, dtype=jnp.int32)
    earlier = (dest_rows[:, None] == dest_rows[None, :]) & (row_ids[None, :] < row_ids[:, None])
    rank_in = jnp.sum(earlier.astype(jnp.int32), axis=1)
    send_slot = dest_rows * capacity + rank_in
    slot_table = jnp.full((device_count * capacity,), -1, jnp.int32).at[send_slot].set(row_ids)
    is_live = slot_table >= 0
    safe_ids = jnp.maximum(slot_table, 0)
    token_ids = safe_ids // top_count
    send_x = jnp.where(is_live[:, None], tokens_in[token_ids], jnp.zeros((), tokens_in.dtype))
    send_dy = jnp.where(is_live[:, None], grad_out[token_ids], jnp.zeros((), grad_out.dtype))
    send_gate = jnp.where(
        is_live, gate_weights.reshape(-1)[safe_ids], jnp.zeros((), gate_weights.dtype)
    )
    block_shape = (group_count, lane_count, capacity, model_width)
    outgoing = (
        send_x.reshape(block_shape),
        send_dy.reshape(block_shape),
        send_gate.reshape(group_count, lane_count, capacity),
    )
    arrived = (
        lax.all_to_all(
            lax.all_to_all(outgoing[0], "ep", split_axis=1, concat_axis=1, tiled=True),
            "grp",
            split_axis=0,
            concat_axis=0,
            tiled=True,
        ),
        lax.all_to_all(
            lax.all_to_all(outgoing[1], "ep", split_axis=1, concat_axis=1, tiled=True),
            "grp",
            split_axis=0,
            concat_axis=0,
            tiled=True,
        ),
        lax.all_to_all(
            lax.all_to_all(outgoing[2], "ep", split_axis=1, concat_axis=1, tiled=True),
            "grp",
            split_axis=0,
            concat_axis=0,
            tiled=True,
        ),
    )
    rows_x = arrived[0].reshape(device_count * capacity, model_width)
    rows_dy = arrived[1].reshape(device_count * capacity, model_width)
    rows_gate = arrived[2].reshape(device_count * capacity)
    row_grad, gate_grad, part_in, part_down = expert_backward(
        rows_x, rows_dy, rows_gate, w_in, w_down
    )
    returning = (
        row_grad.reshape(block_shape),
        gate_grad.reshape(group_count, lane_count, capacity),
    )
    came_back = (
        lax.all_to_all(
            lax.all_to_all(returning[0], "grp", split_axis=0, concat_axis=0, tiled=True),
            "ep",
            split_axis=1,
            concat_axis=1,
            tiled=True,
        ),
        lax.all_to_all(
            lax.all_to_all(returning[1], "grp", split_axis=0, concat_axis=0, tiled=True),
            "ep",
            split_axis=1,
            concat_axis=1,
            tiled=True,
        ),
    )
    grads_rows = came_back[0].reshape(device_count * capacity, model_width)[send_slot]
    d_tokens = jnp.sum(
        grads_rows.reshape(tok_count, top_count, model_width).astype(jnp.float32), axis=1
    ).astype(jnp.bfloat16)
    d_gates = came_back[1].reshape(-1)[send_slot].reshape(tok_count, top_count)
    group_index = lax.axis_index("grp")
    column_index = lax.axis_index("ep")
    my_slot = placement[group_index, column_index]
    slot_mask = (jnp.arange(KPC, dtype=jnp.int32) == my_slot).astype(jnp.float32)
    stack_in = slot_mask[:, None, None] * part_in[None]
    stack_down = slot_mask[:, None, None] * part_down[None]
    summed_in, summed_down = (
        lax.psum_scatter(
            stack_in.astype(jnp.bfloat16), "grp", scatter_dimension=1, tiled=True
        ).astype(jnp.float32),
        lax.psum_scatter(
            stack_down.astype(jnp.bfloat16), "grp", scatter_dimension=1, tiled=True
        ).astype(jnp.float32),
    )
    return (d_tokens, d_gates, summed_in.astype(jnp.bfloat16), summed_down.astype(jnp.bfloat16))


def solution(mesh):
    placed = (
        P(("grp", "ep"), None),
        P(("grp", "ep"), None),
        P(("grp", "ep"), None),
        P(("grp", "ep"), None),
        P(),
        P("grp", "ep", None, None),
        P("grp", "ep", None, None),
    )
    return jax.shard_map(
        shards,
        mesh=mesh,
        in_specs=placed,
        out_specs=(
            P(("grp", "ep"), None),
            P(("grp", "ep"), None),
            P("ep", "grp", None),
            P("ep", "grp", None),
        ),
        check_vma=False,
    )
```

profile of v0, /device:TPU:5, one launch (start us, length us, event | category | flops | bytes accessed | tf_op | source)
XLA Modules:
  0.0 362.5 jit_solution(13869735492718378634)
XLA Ops:
  11.8 3.4 gather_fusion
  15.9 5.8 %all-to-all-start = ((bf16[4,8,16]{2,0,1:T(4,128)(2,1)}), bf16[4,8,16]{2,0,1:T(4,128)(2,1)S(1)}, u32[]{:S(2)}, u32[]{:S(2)}) async-start(bf16[4,8,16]{2,0,1:T(4,128)(2,1)} %copy.68), calls=%async_computation | async-start | bytes 16384 | tf_op jit(solution)/shard_map/all_to_all | solution.py:86
  29.0 4.5 %all-to-all-start.1 = ((bf16[4,8,16]{2,1,0:T(8,128)(2,1)}), bf16[4,8,16]{2,1,0:T(8,128)(2,1)S(1)}, u32[]{:S(2)}, u32[]{:S(2)}) async-start(bf16[4,8,16]{2,1,0:T(8,128)(2,1)} %copy.69), calls=%async_computation.1 | async-start | bytes 16384 | tf_op jit(solution)/shard_map/all_to_all | solution.py:85
  33.4 4.5 %copy_select_fusion = (bf16[4,8,16,2048]{3,2,0,1:T(8,128)(2,1)}, bf16[4,8,16,2048]{3,2,0,1:T(8,128)(2,1)}) fusion(bf16[4,8,16,2048]{3,2,1,0:T(8,128)(2,1)} %bitcast.38, pred[4,8,16]{2,0,1:T(4,128)(4,1)S(1)} %copy.70, bf16[4,8,16,2048]{3,2,1,0:T(8,128)(2,1)} %bitcast.39), kind=kLoop, calls=%fused_computation.22 | loop fusion | flops 2097152 | bytes 8389120 | tf_op jit(solution)/shard_map/jit(_where)/select_n | solution.py:59
  38.0 53.3 %all_to_all.50 = bf16[4,8,16,2048]{3,2,0,1:T(8,128)(2,1)} all-to-all(bf16[4,8,16,2048]{3,2,0,1:T(8,128)(2,1)} %get-tuple-element.29), channel_id=1, replica_groups=mesh['grp'=4,'ep'=8] {'ep'}, dimensions={1} | all-to-all | bytes 4194304 | tf_op jit(solution)/shard_map/all_to_all | solution.py:72
  91.2 4.5 %all-to-all-start.2 = ((bf16[4,8,16,2048]{3,2,0,1:T(8,128)(2,1)}), bf16[4,8,16,2048]{3,2,0,1:T(8,128)(2,1)}, u32[]{:S(2)}, u32[]{:S(2)}) async-start(bf16[4,8,16,2048]{3,2,0,1:T(8,128)(2,1)} %get-tuple-element.30), calls=%async_computation.2 | async-start | bytes 4194304 | tf_op jit(solution)/shard_map/all_to_all | solution.py:79
  98.9 44.4 %all-to-all-done.2 = bf16[4,8,16,2048]{3,2,0,1:T(8,128)(2,1)} async-done(((bf16[4,8,16,2048]{3,2,0,1:T(8,128)(2,1)}), bf16[4,8,16,2048]{3,2,0,1:T(8,128)(2,1)}, u32[]{:S(2)}, u32[]{:S(2)}) %all-to-all-start.2) | async-done | bytes 2097184 | tf_op jit(solution)/shard_map/all_to_all | solution.py:79
  143.3 5.9 %all-to-all-start.5 = ((bf16[4,8,16,2048]{3,2,1,0:T(8,128)(2,1)}), bf16[4,8,16,2048]{3,2,1,0:T(8,128)(2,1)}, u32[]{:S(2)}, u32[]{:S(2)}) async-start(bf16[4,8,16,2048]{3,2,1,0:T(8,128)(2,1)} %copy.74), calls=%async_computation.5 | async-start | bytes 4194304 | tf_op jit(solution)/shard_map/all_to_all | solution.py:71
  152.4 21.7 %all-to-all-done.5 = bf16[4,8,16,2048]{3,2,1,0:T(8,128)(2,1)} async-done(((bf16[4,8,16,2048]{3,2,1,0:T(8,128)(2,1)}), bf16[4,8,16,2048]{3,2,1,0:T(8,128)(2,1)}, u32[]{:S(2)}, u32[]{:S(2)}) %all-to-all-start.5) | async-done | bytes 2097184 | tf_op jit(solution)/shard_map/all_to_all | solution.py:71
  174.1 5.3 %all-to-all-start.3 = ((bf16[4,8,16,2048]{3,2,1,0:T(8,128)(2,1)}), bf16[4,8,16,2048]{3,2,1,0:T(8,128)(2,1)}, u32[]{:S(2)}, u32[]{:S(2)}) async-start(bf16[4,8,16,2048]{3,2,1,0:T(8,128)(2,1)} %copy.72), calls=%async_computation.3 | async-start | bytes 4194304 | tf_op jit(solution)/shard_map/all_to_all | solution.py:78
  181.4 6.5 %fusion.5 = f32[512,1024]{0,1:T(8,128)} fusion(bf16[512,2048]{1,0:T(8,128)(2,1)} %bitcast.6, bf16[1,1,2048,1024]{3,2,1,0:T(8,128)(2,1)} %param.12), kind=kOutput, calls=%fused_computation.16 | convolution fusion | flops 2147483648 | bytes 8388608 | tf_op jit(solution)/shard_map/dot_general | solution.py:11
  187.9 16.4 %all-to-all-done.3 = bf16[4,8,16,2048]{3,2,1,0:T(8,128)(2,1)} async-done(((bf16[4,8,16,2048]{3,2,1,0:T(8,128)(2,1)}), bf16[4,8,16,2048]{3,2,1,0:T(8,128)(2,1)}, u32[]{:S(2)}, u32[]{:S(2)}) %all-to-all-start.3) | async-done | bytes 2097184 | tf_op jit(solution)/shard_map/all_to_all | solution.py:78
  215.5 8.0 %fusion.14 = f32[2048,1024]{1,0:T(8,128)} fusion(bf16[512,2048]{1,0:T(8,128)(2,1)} %bitcast.6, bf16[512,512]{0,1:T(8,128)(2,1)} %get-tuple-element.27, bf16[512,512]{0,1:T(8,128)(2,1)S(1)} %get-tuple-element.26), kind=kOutput, calls=%fused_computation.30 | convolution fusion | flops 2149580800 | bytes 11534336 | tf_op jit(solution)/shard_map/dot_general | solution.py:31
  223.5 9.0 %multiply_convert_fusion = bf16[2,2048,1024]{2,1,0:T(8,128)(2,1)} fusion(f32[2048,1024]{1,0:T(8,128)} %fusion.14, f32[2]{0:T(128)S(1)} %compare_convert_fusion), kind=kLoop, calls=%fused_computation.6 | loop fusion | flops 8388608 | bytes 16777224 | tf_op jit(solution)/shard_map/convert_element_type | solution.py:132
  232.5 3.4 fusion.1
  236.6 3.8 %all-to-all-start.8 = ((bf16[4,8,16]{2,1,0:T(8,128)(2,1)}), bf16[4,8,16]{2,1,0:T(8,128)(2,1)S(1)}, u32[]{:S(2)}, u32[]{:S(2)}) async-start(bf16[4,8,16]{2,1,0:T(8,128)(2,1)} %convert_element_type.77), calls=%async_computation.8 | async-start | bytes 16384 | tf_op jit(solution)/shard_map/all_to_all | solution.py:112
  240.4 6.2 %fusion.7 = bf16[512,2048]{1,0:T(8,128)(2,1)} fusion(bf16[1,1,2048,1024]{3,2,1,0:T(8,128)(2,1)} %param.12, bf16[512,512]{0,1:T(8,128)(2,1)} %get-tuple-element.27, bf16[512,512]{0,1:T(8,128)(2,1)S(1)} %get-tuple-element.26), kind=kOutput, calls=%fused_computation.18 | convolution fusion | flops 2150629376 | bytes 7340032 | tf_op jit(solution)/shard_map/dot_general | solution.py:28
  246.6 4.5 %all-to-all-start.6 = ((bf16[4,8,16,2048]{3,2,1,0:T(8,128)(2,1)}), bf16[4,8,16,2048]{3,2,1,0:T(8,128)(2,1)}, u32[]{:S(2)}, u32[]{:S(2)}) async-start(bf16[4,8,16,2048]{3,2,1,0:T(8,128)(2,1)} %bitcast.40), calls=%async_computation.6 | async-start | bytes 4194304 | tf_op jit(solution)/shard_map/all_to_all | solution.py:105
  251.6 27.9 %all-to-all-done.6 = bf16[4,8,16,2048]{3,2,1,0:T(8,128)(2,1)} async-done(((bf16[4,8,16,2048]{3,2,1,0:T(8,128)(2,1)}), bf16[4,8,16,2048]{3,2,1,0:T(8,128)(2,1)}, u32[]{:S(2)}, u32[]{:S(2)}) %all-to-all-start.6) | async-done | bytes 2097184 | tf_op jit(solution)/shard_map/all_to_all | solution.py:105
  279.5 5.5 %all-to-all-start.9 = ((bf16[4,8,16]{2,0,1:T(4,128)(2,1)}), bf16[4,8,16]{2,0,1:T(4,128)(2,1)S(1)}, u32[]{:S(2)}, u32[]{:S(2)}) async-start(bf16[4,8,16]{2,0,1:T(4,128)(2,1)} %copy.79), calls=%async_computation.9 | async-start | bytes 16384 | tf_op jit(solution)/shard_map/all_to_all | solution.py:111
  289.2 5.4 %all-to-all-start.7 = ((bf16[4,8,16,2048]{3,2,0,1:T(8,128)(2,1)}), bf16[4,8,16,2048]{3,2,0,1:T(8,128)(2,1)}, u32[]{:S(2)}, u32[]{:S(2)}) async-start(bf16[4,8,16,2048]{3,2,0,1:T(8,128)(2,1)} %copy.77), calls=%async_computation.7 | async-start | bytes 4194304 | tf_op jit(solution)/shard_map/all_to_all | solution.py:104
  297.4 44.8 %all-to-all-done.7 = bf16[4,8,16,2048]{3,2,0,1:T(8,128)(2,1)} async-done(((bf16[4,8,16,2048]{3,2,0,1:T(8,128)(2,1)}), bf16[4,8,16,2048]{3,2,0,1:T(8,128)(2,1)}, u32[]{:S(2)}, u32[]{:S(2)}) %all-to-all-start.7) | async-done | bytes 2097184 | tf_op jit(solution)/shard_map/all_to_all | solution.py:104
  345.4 4.2 %gather_fusion.3 = bf16[256,2048]{1,0:T(8,128)(2,1)S(1)} fusion(bf16[512,2048]{1,0:T(8,128)(2,1)} %bitcast.37, s32[1024]{0:T(1024)S(1)} %pad_clamp_fusion), kind=kCustom, calls=%fused_computation.3 | custom fusion | bytes 2098176 | tf_op jit(solution)/shard_map/gather | solution.py:119
  351.1 4.6 %reduce_sum.34 = bf16[128,2048]{1,0:T(8,128)(2,1)} reduce(bf16[128,2,2048]{2,1,0:T(2,128)(2,1)} %reshape.109, bf16[]{:T(256)} %constant.38.clone.1), dimensions={1}, to_apply=%region_2.3 | reduce | flops 262144 | bytes 1572866 | tf_op jit(solution)/shard_map/reduce_sum | solution.py:120
  (61 shorter events, 45.0 us)
Async XLA Ops:
  7.2 199.3 %copy-start = (bf16[1,1,2048,512]{3,2,1,0:T(8,128)(2,1)S(1)}, bf16[1,1,2048,512]{3,2,1,0:T(8,128)(2,1)}, u32[]{:S(2)}) copy-start(bf16[1,1,2048,512]{3,2,1,0:T(8,128)(2,1)} %param.13) | copy-start | bytes 6291460
  7.2 14.6 %copy-start.1 = (bf16[128,2048]{1,0:T(8,128)(2,1)S(1)}, bf16[128,2048]{1,0:T(8,128)(2,1)}, u32[]{:S(2)}) copy-start(bf16[128,2048]{1,0:T(8,128)(2,1)} %param.7) | copy-start | bytes 1572868
  15.9 12.5 %all-to-all-start = ((bf16[4,8,16]{2,0,1:T(4,128)(2,1)}), bf16[4,8,16]{2,0,1:T(4,128)(2,1)S(1)}, u32[]{:S(2)}, u32[]{:S(2)}) async-start(bf16[4,8,16]{2,0,1:T(4,128)(2,1)} %copy.68), calls=%async_computation | async-start | bytes 16384 | tf_op jit(solution)/shard_map/all_to_all | solution.py:86
  21.8 3.3 copy-start.2
  29.0 9.0 %all-to-all-start.1 = ((bf16[4,8,16]{2,1,0:T(8,128)(2,1)}), bf16[4,8,16]{2,1,0:T(8,128)(2,1)S(1)}, u32[]{:S(2)}, u32[]{:S(2)}) async-start(bf16[4,8,16]{2,1,0:T(8,128)(2,1)} %copy.69), calls=%async_computation.1 | async-start | bytes 16384 | tf_op jit(solution)/shard_map/all_to_all | solution.py:85
  91.2 52.1 %all-to-all-start.2 = ((bf16[4,8,16,2048]{3,2,0,1:T(8,128)(2,1)}), bf16[4,8,16,2048]{3,2,0,1:T(8,128)(2,1)}, u32[]{:S(2)}, u32[]{:S(2)}) async-start(bf16[4,8,16,2048]{3,2,0,1:T(8,128)(2,1)} %get-tuple-element.30), calls=%async_computation.2 | async-start | bytes 4194304 | tf_op jit(solution)/shard_map/all_to_all | solution.py:79
  143.3 30.8 %all-to-all-start.5 = ((bf16[4,8,16,2048]{3,2,1,0:T(8,128)(2,1)}), bf16[4,8,16,2048]{3,2,1,0:T(8,128)(2,1)}, u32[]{:S(2)}, u32[]{:S(2)}) async-start(bf16[4,8,16,2048]{3,2,1,0:T(8,128)(2,1)} %copy.74), calls=%async_computation.5 | async-start | bytes 4194304 | tf_op jit(solution)/shard_map/all_to_all | solution.py:71
  174.1 30.2 %all-to-all-start.3 = ((bf16[4,8,16,2048]{3,2,1,0:T(8,128)(2,1)}), bf16[4,8,16,2048]{3,2,1,0:T(8,128)(2,1)}, u32[]{:S(2)}, u32[]{:S(2)}) async-start(bf16[4,8,16,2048]{3,2,1,0:T(8,128)(2,1)} %copy.72), calls=%async_computation.3 | async-start | bytes 4194304 | tf_op jit(solution)/shard_map/all_to_all | solution.py:78
  179.4 176.3 %reduce-scatter.5.cloned.1.call-start = ((), (), s32[]{:S(2)}) async-start(), calls=%async_computation.13 | async-start | bytes 5242880 | tf_op jit(solution)/shard_map/reduce_scatter | solution.py:134
  204.3 2.2 copy-start.3
  215.2 140.5 %reduce-scatter.3.cloned.1.call-start = ((), (), s32[]{:S(2)}) async-start(), calls=%async_computation.12 | async-start | bytes 10485760 | tf_op jit(solution)/shard_map/reduce_scatter | solution.py:131
  236.6 9.9 %all-to-all-start.8 = ((bf16[4,8,16]{2,1,0:T(8,128)(2,1)}), bf16[4,8,16]{2,1,0:T(8,128)(2,1)S(1)}, u32[]{:S(2)}, u32[]{:S(2)}) async-start(bf16[4,8,16]{2,1,0:T(8,128)(2,1)} %convert_element_type.77), calls=%async_computation.8 | async-start | bytes 16384 | tf_op jit(solution)/shard_map/all_to_all | solution.py:112
  246.6 33.0 %all-to-all-start.6 = ((bf16[4,8,16,2048]{3,2,1,0:T(8,128)(2,1)}), bf16[4,8,16,2048]{3,2,1,0:T(8,128)(2,1)}, u32[]{:S(2)}, u32[]{:S(2)}) async-start(bf16[4,8,16,2048]{3,2,1,0:T(8,128)(2,1)} %bitcast.40), calls=%async_computation.6 | async-start | bytes 4194304 | tf_op jit(solution)/shard_map/all_to_all | solution.py:105
  279.5 9.7 %all-to-all-start.9 = ((bf16[4,8,16]{2,0,1:T(4,128)(2,1)}), bf16[4,8,16]{2,0,1:T(4,128)(2,1)S(1)}, u32[]{:S(2)}, u32[]{:S(2)}) async-start(bf16[4,8,16]{2,0,1:T(4,128)(2,1)} %copy.79), calls=%async_computation.9 | async-start | bytes 16384 | tf_op jit(solution)/shard_map/all_to_all | solution.py:111
  289.2 53.0 %all-to-all-start.7 = ((bf16[4,8,16,2048]{3,2,0,1:T(8,128)(2,1)}), bf16[4,8,16,2048]{3,2,0,1:T(8,128)(2,1)}, u32[]{:S(2)}, u32[]{:S(2)}) async-start(bf16[4,8,16,2048]{3,2,0,1:T(8,128)(2,1)} %copy.77), calls=%async_computation.7 | async-start | bytes 4194304 | tf_op jit(solution)/shard_map/all_to_all | solution.py:104
Sparse Core Ops, SparseCore 0:
  215.3 45.7 reduce-scatter.4
  264.4 74.2 reduce-scatter.2
where the time goes:
time: 366 us; the launch traced here: 363 us
  waiting for transfers between devices  156 us (43%)
  blocking collectives  53.3 us (15%)
  starting transfers between devices  45.4 us (12%)
  local copies, waits for them, and re-layouts  38.8 us (11%)
  matrix products  27.9 us (8%)
  other arithmetic  26.7 us (7%)
  between operations  14.2 us (4%)
    all_to_all x1, blocking collectives, shards(): lax.all_to_all(outgoing[0], 'ep', split_axis=1, concat_axis=1, tiled=True)  53.3 us
    all_to_all x1, waiting for transfers between devices, shards(): lax.all_to_all(lax.all_to_all(returning[0], 'grp', split_axis=0, concat_a...  44.8 us
    all_to_all x1, waiting for transfers between devices, shards(): lax.all_to_all(outgoing[1], 'ep', split_axis=1, concat_axis=1, tiled=True)  44.4 us
    all_to_all x1, waiting for transfers between devices, shards(): lax.all_to_all(returning[0], 'grp', split_axis=0, concat_axis=0, tiled=True)  27.9 us
    all_to_all x1, waiting for transfers between devices, shards(): lax.all_to_all(lax.all_to_all(outgoing[0], 'ep', split_axis=1, concat_axi...  21.7 us
    all_to_all x1, waiting for transfers between devices, shards(): lax.all_to_all(lax.all_to_all(outgoing[1], 'ep', split_axis=1, concat_axi...  16.4 us
    convert_element_type x1, other arithmetic, shards(): stack_in.astype(jnp.bfloat16)  8.98 us
    dot_general x1, matrix products, expert_backward(): lax.dot_general(rows_x, both_grad, (((0,), (0,)), ((), ())), preferred_el...  8.05 us
  transfers between devices with their start and end apart: 11, of which 6 were waited for; matrix products, arithmetic and copies ran while one was open for 20% of the time, Pallas kernels for 0%

commit v1 on v0

--- a/solution.py
+++ b/solution.py
@@ -1,9 +1,250 @@
+import functools
+
 import jax
 import jax.numpy as jnp
 from jax import lax
+from jax.experimental import pallas as pl
+from jax.experimental.pallas import tpu as pltpu
 from jax.sharding import PartitionSpec as P
 
 KPC = 2
+MESH = pl.DeviceIdType.MESH
+F32 = jnp.float32
+BF16 = jnp.bfloat16
+PIECES = 4
+
+
+def dispatch_kernel(groups, lanes, inner, cap, tok_ref, rows_ref, held, picked,
+                    up_send, down_send, chain_recv, plane_send, plane_recv, own_sem):
+    tok_count, width = tok_ref.shape
+    outer = lanes // inner
+    plane = groups * inner
+    my_group = lax.axis_index("grp")
+    my_lane = lax.axis_index("ep")
+    layer = my_lane // inner
+    within = lax.rem(my_lane, inner)
+    my_seat = my_group * inner + within
+    step_rows = tok_count // PIECES
+
+    def seat_id(seat):
+        return (seat // inner, layer * inner + lax.rem(seat, inner))
+
+    barrier = pltpu.get_barrier_semaphore()
+
+    @pl.loop(1, plane)
+    def _(off):
+        pl.semaphore_signal(barrier, inc=1, device_id=seat_id(lax.rem(my_seat + off, plane)),
+                            device_id_type=MESH)
+
+    @pl.when(layer > 0)
+    def _():
+        pl.semaphore_signal(barrier, inc=1, device_id=(my_group, my_lane - inner),
+                            device_id_type=MESH)
+
+    @pl.when(layer < outer - 1)
+    def _():
+        pl.semaphore_signal(barrier, inc=1, device_id=(my_group, my_lane + inner),
+                            device_id_type=MESH)
+
+    ends = (layer > 0).astype(jnp.int32) + (layer < outer - 1).astype(jnp.int32)
+    pl.semaphore_wait(barrier, plane - 1 + ends)
+
+    def piece(source, part):
+        return held.at[source, pl.ds(part * step_rows, step_rows)]
+
+    def hop(source, part, upward, own):
+        src = tok_ref.at[pl.ds(part * step_rows, step_rows)] if own else piece(source, part)
+        sems = up_send if upward else down_send
+        return pltpu.make_async_remote_copy(
+            src_ref=src,
+            dst_ref=piece(source, part),
+            send_sem=sems.at[source, part],
+            recv_sem=chain_recv.at[source, part],
+            device_id=(my_group, my_lane + inner if upward else my_lane - inner),
+            device_id_type=MESH,
+        )
+
+    def start_hops(source, part, own, come_up, come_down):
+        if come_up:
+            @pl.when(layer < outer - 1)
+            def _():
+                hop(source, part, True, own).start()
+        if come_down:
+            @pl.when(layer > 0)
+            def _():
+                hop(source, part, False, own).start()
+
+    def spread(source, off):
+        seat = lax.rem(my_seat + off, plane)
+        return pltpu.make_async_remote_copy(
+            src_ref=picked.at[source, seat],
+            dst_ref=rows_ref.at[source, my_seat],
+            send_sem=plane_send.at[source, off],
+            recv_sem=plane_recv.at[source, off],
+            device_id=seat_id(seat),
+            device_id_type=MESH,
+        )
+
+    def own_copy(source):
+        return pltpu.make_async_copy(
+            picked.at[source, my_seat], rows_ref.at[source, my_seat], own_sem.at[source]
+        )
+
+    def pick(source, view):
+        facts = view[:, width - 128:].astype(F32).T
+        slots = lax.broadcasted_iota(jnp.int32, (plane * cap, tok_count), 0).astype(F32)
+        here = layer.astype(F32)
+        first = ((facts[2:3] == here) & (facts[4:5] == slots)).astype(F32)
+        second = ((facts[3:4] == here) & (facts[5:6] == slots)).astype(F32)
+        chosen = (first + second).astype(BF16)
+        step = 1024
+        for begin in range(0, width - 128, step):
+            got = jnp.dot(chosen, view[:, begin:begin + step], preferred_element_type=F32)
+            picked[source, :, :, begin:begin + step] = got.astype(BF16).reshape(plane, cap, step)
+        weights = jnp.sum(first * facts[0:1] + second * facts[1:2], axis=1, keepdims=True)
+        tail = jnp.broadcast_to(weights, (plane * cap, 128)).astype(BF16)
+        picked[source, :, :, width - 128:] = tail.reshape(plane, cap, 128)
+        own_copy(source).start()
+
+        @pl.loop(1, plane)
+        def _(off):
+            spread(source, off).start()
+
+    for part in range(PIECES):
+        start_hops(layer, part, True, True, True)
+    pick(layer, tok_ref)
+    for far in range(1, outer):
+        below = layer - far
+        above = layer + far
+        for part in range(PIECES):
+            @pl.when(below >= 0)
+            def _():
+                hop(below, part, True, False).wait_recv()
+                start_hops(below, part, False, True, False)
+
+            @pl.when(above < outer)
+            def _():
+                hop(above, part, False, False).wait_recv()
+                start_hops(above, part, False, False, True)
+
+        @pl.when(below >= 0)
+        def _():
+            pick(below, held.at[below])
+
+        @pl.when(above < outer)
+        def _():
+            pick(above, held.at[above])
+
+    for source in range(outer):
+        own_copy(source).wait()
+
+        @pl.loop(1, plane)
+        def _(off):
+            spread(source, off).wait_recv()
+            spread(source, off).wait_send()
+
+        for part in range(PIECES):
+            @pl.when((source <= layer) & (layer < outer - 1))
+            def _():
+                hop(source, part, True, False).wait_send()
+
+            @pl.when((source >= layer) & (layer > 0))
+            def _():
+                hop(source, part, False, False).wait_send()
+
+
+def return_kernel(groups, lanes, inner, cap, slots_ref, rows_ref, in_ref, down_ref,
+                  tokens_ref, gates_ref, got_in, got_down,
+                  back, row_send, row_recv, in_send, in_recv, down_send, down_recv, own_sem):
+    tok_count = slots_ref.shape[0]
+    width = rows_ref.shape[-1]
+    devices = groups * lanes
+    my_group = lax.axis_index("grp")
+    my_lane = lax.axis_index("ep")
+    me = my_group * lanes + my_lane
+
+    barrier = pltpu.get_barrier_semaphore()
+
+    @pl.loop(1, devices)
+    def _(off):
+        peer = lax.rem(me + off, devices)
+        pl.semaphore_signal(barrier, inc=1, device_id=(peer // lanes, lax.rem(peer, lanes)),
+                            device_id_type=MESH)
+
+    pl.semaphore_wait(barrier, devices - 1)
+
+    def row_copy(off):
+        peer = lax.rem(me + off, devices)
+        group = peer // lanes
+        lane = lax.rem(peer, lanes)
+        return pltpu.make_async_remote_copy(
+            src_ref=rows_ref.at[lane // inner, group * inner + lax.rem(lane, inner)],
+            dst_ref=back.at[me],
+            send_sem=row_send.at[off],
+            recv_sem=row_recv.at[off],
+            device_id=(group, lane),
+            device_id_type=MESH,
+        )
+
+    def sum_copy(src, dst, send, recv, off):
+        group = lax.rem(my_group + off, groups)
+        return pltpu.make_async_remote_copy(
+            src_ref=src.at[group],
+            dst_ref=dst.at[my_group],
+            send_sem=send.at[off],
+            recv_sem=recv.at[off],
+            device_id=(group, my_lane),
+            device_id_type=MESH,
+        )
+
+    own = [
+        pltpu.make_async_copy(
+            rows_ref.at[my_lane // inner, my_group * inner + lax.rem(my_lane, inner)],
+            back.at[me], own_sem.at[0]),
+        pltpu.make_async_copy(in_ref.at[my_group], got_in.at[my_group], own_sem.at[1]),
+        pltpu.make_async_copy(down_ref.at[my_group], got_down.at[my_group], own_sem.at[2]),
+    ]
+
+    @pl.loop(1, devices)
+    def _(off):
+        row_copy(off).start()
+
+    for off in range(1, groups):
+        sum_copy(in_ref, got_in, in_send, in_recv, off).start()
+        sum_copy(down_ref, got_down, down_send, down_recv, off).start()
+    for copy in own:
+        copy.start()
+
+    own[0].wait()
+
+    @pl.loop(1, devices)
+    def _(off):
+        row_copy(off).wait_recv()
+
+    places = lax.broadcasted_iota(jnp.int32, (tok_count, devices * cap), 1)
+    first = (slots_ref[:, 0:1] == places).astype(F32)
+    second = (slots_ref[:, 1:2] == places).astype(F32)
+    both = (first + second).astype(BF16)
+    step = 512
+    for begin in range(0, width - 128, step):
+        view = back[:, :, begin:begin + step].reshape(devices * cap, step)
+        tokens_ref[:, begin:begin + step] = jnp.dot(
+            both, view, preferred_element_type=F32).astype(BF16)
+    tail = back[:, :, width - 128:].reshape(devices * cap, 128)
+    gate_first = jnp.dot(first.astype(BF16), tail, preferred_element_type=F32)
+    gate_second = jnp.dot(second.astype(BF16), tail, preferred_element_type=F32)
+    lane_ids = lax.broadcasted_iota(jnp.int32, (tok_count, 128), 1)
+    gates_ref[...] = jnp.where(lane_ids == 0, gate_first, gate_second).astype(BF16)
+
+    own[1].wait()
+    own[2].wait()
+    for off in range(1, groups):
+        sum_copy(in_ref, got_in, in_send, in_recv, off).wait()
+        sum_copy(down_ref, got_down, down_send, down_recv, off).wait()
+
+    @pl.loop(1, devices)
+    def _(off):
+        row_copy(off).wait_send()
 
 
 def expert_backward(rows_x, rows_dy, rows_gate, w_in, w_down):
@@ -37,7 +278,7 @@
     return (row_grad, gate_grad, part_in, part_down)
 
 
-def shards(tokens_in, grad_out, replica_of, gate_weights, placement, w_in_rep, w_down_rep):
+def plain_shards(tokens_in, grad_out, replica_of, gate_weights, placement, w_in_rep, w_down_rep):
     tok_count, model_width = tokens_in.shape
     top_count = replica_of.shape[1]
     group_count = lax.axis_size("grp")
@@ -138,6 +379,110 @@
     return (d_tokens, d_gates, summed_in.astype(jnp.bfloat16), summed_down.astype(jnp.bfloat16))
 
 
+def shards(tokens_in, grad_out, replica_of, gate_weights, placement, w_in_rep, w_down_rep):
+    tok_count, width = tokens_in.shape
+    top_count = replica_of.shape[1]
+    groups = lax.axis_size("grp")
+    lanes = lax.axis_size("ep")
+    devices = groups * lanes
+    cap = max(2, 2 * tok_count * top_count // devices)
+    if cap % 16 or top_count != 2:
+        return plain_shards(
+            tokens_in, grad_out, replica_of, gate_weights, placement, w_in_rep, w_down_rep
+        )
+    inner = max(1, min(lanes, tok_count // (groups * cap)))
+    outer = lanes // inner
+    plane = groups * inner
+    w_in = w_in_rep[0, 0]
+    w_down = w_down_rep[0, 0]
+    hidden = w_down.shape[1]
+    dest_rows = replica_of.reshape(-1)
+    row_ids = jnp.arange(tok_count * top_count, dtype=jnp.int32)
+    earlier = (dest_rows[:, None] == dest_rows[None, :]) & (row_ids[None, :] < row_ids[:, None])
+    rank_in = jnp.sum(earlier.astype(jnp.int32), axis=1).reshape(tok_count, top_count)
+    lane_of = replica_of % lanes
+    seat_of = replica_of // lanes * inner + lane_of % inner
+    facts = jnp.concatenate(
+        [
+            gate_weights,
+            (lane_of // inner).astype(BF16),
+            (seat_of * cap + rank_in).astype(BF16),
+            jnp.zeros((tok_count, 128 - 3 * top_count), BF16),
+        ],
+        axis=1,
+    )
+    tok = jnp.concatenate([tokens_in, grad_out, facts], axis=1)
+    full = tok.shape[1]
+    any_spec = pl.BlockSpec(memory_space=pl.ANY)
+    vmem_spec = pl.BlockSpec(memory_space=pltpu.VMEM)
+    dma = pltpu.SemaphoreType.DMA
+    rows = pl.pallas_call(
+        functools.partial(dispatch_kernel, groups, lanes, inner, cap),
+        out_shape=jax.ShapeDtypeStruct((outer, plane, cap, full), BF16),
+        in_specs=[vmem_spec],
+        out_specs=any_spec,
+        scratch_shapes=[
+            pltpu.VMEM((outer, tok_count, full), BF16),
+            pltpu.VMEM((outer, plane, cap, full), BF16),
+            dma((outer, PIECES)),
+            dma((outer, PIECES)),
+            dma((outer, PIECES)),
+            dma((outer, plane)),
+            dma((outer, plane)),
+            dma((outer,)),
+        ],
+        compiler_params=pltpu.CompilerParams(
+            collective_id=0, has_side_effects=True, vmem_limit_bytes=40 * 2**20
+        ),
+        name="dispatch",
+    )(tok)
+    row_total = devices * cap
+    rows = rows.reshape(row_total, full)
+    row_grad, gate_grad, part_in, part_down = expert_backward(
+        rows[:, :width], rows[:, width:2 * width], rows[:, 2 * width], w_in, w_down
+    )
+    returned = jnp.concatenate(
+        [row_grad, jnp.broadcast_to(gate_grad[:, None], (row_total, 128))], axis=1
+    ).reshape(outer, plane, cap, width + 128)
+    share = width // groups
+    d_tokens, gates, got_in, got_down = pl.pallas_call(
+        functools.partial(return_kernel, groups, lanes, inner, cap),
+        out_shape=(
+            jax.ShapeDtypeStruct((tok_count, width), BF16),
+            jax.ShapeDtypeStruct((tok_count, 128), BF16),
+            jax.ShapeDtypeStruct((groups, share, 2 * hidden), BF16),
+            jax.ShapeDtypeStruct((groups, share, hidden), BF16),
+        ),
+        in_specs=[vmem_spec, any_spec, any_spec, any_spec],
+        out_specs=(vmem_spec, vmem_spec, any_spec, any_spec),
+        scratch_shapes=[
+            pltpu.VMEM((devices, cap, width + 128), BF16),
+            dma((devices,)),
+            dma((devices,)),
+            dma((groups,)),
+            dma((groups,)),
+            dma((groups,)),
+            dma((groups,)),
+            dma((3,)),
+        ],
+        compiler_params=pltpu.CompilerParams(
+            collective_id=1, has_side_effects=True, vmem_limit_bytes=40 * 2**20
+        ),
+        name="give_back",
+    )(
+        replica_of * cap + rank_in,
+        returned,
+        part_in.astype(BF16).reshape(groups, share, 2 * hidden),
+        part_down.astype(BF16).reshape(groups, share, hidden),
+    )
+    column = placement[:, lax.axis_index("ep")]
+    mask = (column[None, :] == jnp.arange(KPC, dtype=jnp.int32)[:, None])[:, :, None, None]
+    zero = jnp.zeros((), F32)
+    summed_in = jnp.sum(jnp.where(mask, got_in[None].astype(F32), zero), axis=1)
+    summed_down = jnp.sum(jnp.where(mask, got_down[None].astype(F32), zero), axis=1)
+    return d_tokens, gates[:, :top_count], summed_in.astype(BF16), summed_down.astype(BF16)
+
+
 def solution(mesh):
     placed = (
         P(("grp", "ep"), None),

time: 366 us -> 225 us (0.61)
  Pallas kernels: 0 us -> 187 us
  waiting for transfers between devices: 156 us -> 0 us
  blocking collectives: 53.3 us -> 0 us
  starting transfers between devices: 45.4 us -> 0 us
  local copies, waits for them, and re-layouts: 38.8 us -> 6.34 us
  matrix products: 27.9 us -> 13.8 us
  between operations: 14.2 us -> 0.78 us
  other arithmetic: 26.7 us -> 15.8 us
    pallas_call x0 -> x2, Pallas kernels: none -> 187 us  [the longest x1 97.8 us: shards(): pl.pallas_call(functools.partial(return_kernel, groups, lanes, inner, cap...]
    all_to_all x9 -> x0, waiting for transfers between devices: 156 us -> none  [the longest x1 44.8 us: shards(): lax.all_to_all(lax.all_to_all(returning[0], 'grp', split_axis=0, concat_a...]
    all_to_all x1 -> x0, blocking collectives: 53.3 us -> none  [shards(): lax.all_to_all(outgoing[0], 'ep', split_axis=1, concat_axis=1, tiled=True)]
    all_to_all x9 -> x0, starting transfers between devices: 45.1 us -> none  [the longest x1 5.88 us: shards(): lax.all_to_all(lax.all_to_all(outgoing[0], 'ep', split_axis=1, concat_axi...]
    gather x5 -> x0, local copies, waits for them, and re-layouts: 16.1 us -> none  [the longest x1 4.22 us: shards(): came_back[0].reshape(device_count * capacity, model_width)[send_slot]]
    all_to_all x7 -> x0, local copies, waits for them, and re-layouts: 13.9 us -> none  [the longest x1 3.19 us: shards(): lax.all_to_all(outgoing[1], 'ep', split_axis=1, concat_axis=1, tiled=True)]
    convert_element_type x6 -> x3, other arithmetic: 16.6 us -> 5.01 us  [the longest x1 4.29 us: shards(): summed_in = jnp.sum(jnp.where(mask, got_in[None].astype(F32), zero), axis=1)]
    select_n x3 -> x0, other arithmetic: 4.54 us -> none  [the longest x1 4.52 us: shards(): jnp.where(is_live[:, None], tokens_in[token_ids], jnp.zeros((), tokens_in...]
  transfers between devices with their start and end apart: 11 -> 0, of which waited for: 6 -> 0; matrix products, arithmetic and copies ran while one was open for 20% -> 0% of each run, Pallas kernels for 0% -> 0%
where the time goes in v1:
time: 225 us; the launch traced here: 224 us
  Pallas kernels  187 us (83%)
  other arithmetic  15.8 us (7%)
  matrix products  13.8 us (6%)
  local copies, waits for them, and re-layouts  6.34 us (3%)
    pallas_call x1, Pallas kernels, shards(): pl.pallas_call(functools.partial(return_kernel, groups, lanes, inner, cap...  97.8 us
    pallas_call x1, Pallas kernels, shards(): pl.pallas_call(functools.partial(dispatch_kernel, groups, lanes, inner, c...  89.1 us
    reduce_sum x1, other arithmetic, shards(): summed_in = jnp.sum(jnp.where(mask, got_in[None].astype(F32), zero), axis=1)  6.87 us

profile of v1, /device:TPU:5, one launch (start us, length us, event | category | flops | bytes accessed | tf_op | source)
XLA Modules:
  0.0 223.7 jit_solution(16776603120606489569)
XLA Ops:
  0.6 0.9 copy.52
  1.7 0.2 convert_reduce_fusion.1
  1.9 0.1 reshape.52
  2.1 0.7 broadcast_multiply_fusion
  2.9 0.7 broadcast_compare_fusion
  3.7 0.1 fusion.23
  3.8 0.8 copy.62
  4.6 2.3 %concatenate.10.tok_ref = bf16[128,4224]{1,0:T(8,128)(2,1)S(1)} concatenate(bf16[128,2048]{1,0:T(8,128)(2,1)} %param.7, bf16[128,2048]{1,0:T(8,128)(2,1)} %param.8, bf16[128,2]{1,0:T(8,128)(2,1)S(1)} %copy.62, bf16[128,2]{1,0:T(8,128)(2,1)S(1)} %get-tuple-element.32, bf16[128,2]{1,0:T(8,128)(2,1)S(1)} %get-tuple-element.31, bf16[128,122]{1,0:T(8,128)(2,1)S(1)} %broadcast_in_dim.56), dimensions={1} | concatenate | bytes 2162688 | tf_op jit(solution)/shard_map/concatenate | solution.py:414
  7.0 89.1 %dispatch.1 = bf16[4,8,16,4224]{3,2,1,0:T(8,128)(2,1)S(1)} custom-call(bf16[128,4224]{1,0:T(8,128)(2,1)S(1)} %concatenate.10.tok_ref), custom_call_target="tpu_custom_call" | custom-call | tf_op jit(solution)/shard_map/dispatch/pallas_call | solution.py:419
  96.2 2.4 %fusion.4 = f32[512,1024]{0,1:T(8,128)S(1)} fusion(bf16[1,1,2048,1024]{3,2,1,0:T(8,128)(2,1)S(1)} %copy-done.4, bf16[512,4224]{1,0:T(8,128)(2,1)S(1)} %bitcast.23), kind=kOutput, calls=%fused_computation.8 | convolution fusion | flops 2147483648 | bytes 8388608 | tf_op jit(solution)/shard_map/dot_general | solution.py:252
  98.6 1.8 multiply_convert_fusion.2
  100.4 1.5 convolution_convert_fusion.1
  101.9 4.3 %convolution_convert_fusion = bf16[2048,1024]{1,0:T(8,128)(2,1)} fusion(bf16[512,4224]{1,0:T(8,128)(2,1)S(1)} %bitcast.26, bf16[512,512]{0,1:T(8,128)(2,1)S(1)} %get-tuple-element.29, bf16[512,512]{0,1:T(8,128)(2,1)S(1)} %get-tuple-element.28), kind=kOutput, calls=%fused_computation.10 | convolution fusion | flops 2151677952 | bytes 7340032 | tf_op jit(solution)/shard_map/dot_general | solution.py:272
  106.2 2.4 %fusion.6 = bf16[512,2048]{1,0:T(8,128)(2,1)S(1)} fusion(bf16[1,1,2048,1024]{3,2,1,0:T(8,128)(2,1)S(1)} %copy-done.4, bf16[512,512]{0,1:T(8,128)(2,1)S(1)} %get-tuple-element.29, bf16[512,512]{0,1:T(8,128)(2,1)S(1)} %get-tuple-element.28), kind=kOutput, calls=%fused_computation.11 | convolution fusion | flops 2150629376 | bytes 7340032 | tf_op jit(solution)/shard_map/dot_general | solution.py:269
  108.7 1.4 fusion.1
  110.2 0.4 pad_maximum_fusion
  110.6 97.8 %give_back.1 = (bf16[128,2048]{1,0:T(8,128)(2,1)S(1)}, bf16[128,128]{1,0:T(8,128)(2,1)S(1)}, bf16[4,512,1024]{2,1,0:T(8,128)(2,1)S(1)}, bf16[4,512,512]{2,1,0:T(8,128)(2,1)S(1)}) custom-call(s32[128,2]{1,0:T(8,128)S(1)} %get-tuple-element.33.slots_ref, bf16[4,8,16,2176]{3,2,1,0:T(8,128)(2,1)S(1)} %bitcast.21, bf16[4,512,1024]{2,1,0:T(8,128)(2,1)} %bitcast.30, ...), custom_call_target="tpu_custom_call" | custom-call | tf_op jit(solution)/shard_map/give_back/pallas_call | solution.py:448
  208.5 4.3 %convert_element_type.62 = f32[4,512,1024]{2,1,0:T(8,128)} convert(bf16[4,512,1024]{2,1,0:T(8,128)(2,1)S(1)} %get-tuple-element.10) | non-fusion elementwise | flops 2097152 | bytes 12582912 | tf_op jit(solution)/shard_map/convert_element_type | solution.py:481
  212.8 0.2 dynamic-slice_reduce_fusion
  213.0 6.9 %select_reduce_fusion = bf16[2,512,1024]{2,1,0:T(8,128)(2,1)} fusion(f32[4,512,1024]{2,1,0:T(8,128)} %convert_element_type.62, pred[2,4]{1,0:T(4,128)(4,1)S(1)} %iota_compare_fusion.1), kind=kLoop, calls=%fused_computation | loop fusion | flops 7340032 | bytes 10485768 | tf_op jit(solution)/shard_map/reduce_sum | solution.py:481
  219.9 0.6 convert_element_type.64
  220.5 1.8 select_reduce_fusion.1
  222.3 0.6 copy.65
  222.9 0.8 copy.71
  (17 shorter events, 0.7 us)
Async XLA Ops:
  0.6 98.0 %copy-start = (bf16[1,1,2048,512]{3,2,1,0:T(8,128)(2,1)S(1)}, bf16[1,1,2048,512]{3,2,1,0:T(8,128)(2,1)}, u32[]{:S(2)}) copy-start(bf16[1,1,2048,512]{3,2,1,0:T(8,128)(2,1)} %param.13) | copy-start | bytes 6291460
  7.0 89.3 %copy-start.4 = (bf16[1,1,2048,1024]{3,2,1,0:T(8,128)(2,1)S(1)}, bf16[1,1,2048,1024]{3,2,1,0:T(8,128)(2,1)}, u32[]{:S(2)}) copy-start(bf16[1,1,2048,1024]{3,2,1,0:T(8,128)(2,1)} %param.12) | copy-start | bytes 12582916
  208.5 4.3 %copy-start.1 = (bf16[4,512,512]{2,1,0:T(8,128)(2,1)}, bf16[4,512,512]{2,1,0:T(8,128)(2,1)S(1)}, u32[]{:S(2)}) copy-start(bf16[4,512,512]{2,1,0:T(8,128)(2,1)S(1)} %get-tuple-element.11) | copy-start | bytes 6291460
  208.5 4.3 %copy-start.3 = (s32[4,8]{1,0:T(4,128)S(1)}, s32[4,8]{1,0:T(4,128)}, u32[]{:S(2)}) copy-start(s32[4,8]{1,0:T(4,128)} %param.11) | copy-start | bytes 388
  213.0 6.9 %copy-start.2 = (bf16[4,512,512]{2,1,0:T(8,128)(2,1)S(1)}, bf16[4,512,512]{2,1,0:T(8,128)(2,1)}, u32[]{:S(2)}) copy-start(bf16[4,512,512]{2,1,0:T(8,128)(2,1)} %copy-done.1) | copy-start | bytes 6291460

commit v2 on v0

--- a/solution.py
+++ b/solution.py
@@ -1,9 +1,310 @@
+import functools
+
 import jax
 import jax.numpy as jnp
 from jax import lax
+from jax.experimental import pallas as pl
+from jax.experimental.pallas import tpu as pltpu
 from jax.sharding import PartitionSpec as P
 
 KPC = 2
+MESH = pl.DeviceIdType.MESH
+F32 = jnp.float32
+BF16 = jnp.bfloat16
+PIECES = 4
+
+
+def layer_kernel(groups, lanes, inner, cap, tok_ref, slots_ref, mask_ref, w_in_hbm, w_down_hbm,
+                 tokens_ref, gates_ref, grad_in_ref, grad_down_ref,
+                 held, picked, rows, w_in, w_down, both_grads, gated, row_grads, back,
+                 part_in, part_down, got_in, got_down,
+                 up_send, down_send, chain_recv, plane_send, plane_recv, own_sem, load_sem,
+                 row_send, row_recv, row_own, in_send, in_recv, down_sent, down_recv):
+    tok_count, full = tok_ref.shape
+    width = (full - 128) // 2
+    hidden = w_down.shape[1]
+    outer = lanes // inner
+    plane = groups * inner
+    devices = groups * lanes
+    batch = plane * cap
+    share = width // groups
+    my_group = lax.axis_index("grp")
+    my_lane = lax.axis_index("ep")
+    me = my_group * lanes + my_lane
+    layer = my_lane // inner
+    my_seat = my_group * inner + lax.rem(my_lane, inner)
+    step_rows = tok_count // PIECES
+
+    load_in = pltpu.make_async_copy(w_in_hbm, w_in, load_sem.at[0])
+    load_down = pltpu.make_async_copy(w_down_hbm, w_down, load_sem.at[1])
+    load_in.start()
+    load_down.start()
+
+    barrier = pltpu.get_barrier_semaphore()
+
+    @pl.loop(1, devices)
+    def _(off):
+        peer = lax.rem(me + off, devices)
+        pl.semaphore_signal(barrier, inc=1, device_id=(peer // lanes, lax.rem(peer, lanes)),
+                            device_id_type=MESH)
+
+    pl.semaphore_wait(barrier, devices - 1)
+
+    def piece(source, part):
+        return held.at[source, pl.ds(part * step_rows, step_rows)]
+
+    def hop(source, part, upward, own):
+        src = tok_ref.at[pl.ds(part * step_rows, step_rows)] if own else piece(source, part)
+        sems = up_send if upward else down_send
+        return pltpu.make_async_remote_copy(
+            src_ref=src,
+            dst_ref=piece(source, part),
+            send_sem=sems.at[source, part],
+            recv_sem=chain_recv.at[source, part],
+            device_id=(my_group, my_lane + inner if upward else my_lane - inner),
+            device_id_type=MESH,
+        )
+
+    def spread(source, off):
+        seat = lax.rem(my_seat + off, plane)
+        return pltpu.make_async_remote_copy(
+            src_ref=picked.at[source, seat],
+            dst_ref=rows.at[source, my_seat],
+            send_sem=plane_send.at[source, off],
+            recv_sem=plane_recv.at[source, off],
+            device_id=(seat // inner, layer * inner + lax.rem(seat, inner)),
+            device_id_type=MESH,
+        )
+
+    def own_copy(source):
+        return pltpu.make_async_copy(
+            picked.at[source, my_seat], rows.at[source, my_seat], own_sem.at[source]
+        )
+
+    def row_copy(source, seat):
+        return pltpu.make_async_remote_copy(
+            src_ref=row_grads.at[source, seat],
+            dst_ref=back.at[me],
+            send_sem=row_send.at[source, seat],
+            recv_sem=row_recv.at[me],
+            device_id=(seat // inner, source * inner + lax.rem(seat, inner)),
+            device_id_type=MESH,
+        )
+
+    def row_arrival(peer):
+        return pltpu.make_async_remote_copy(
+            src_ref=row_grads.at[0, 0],
+            dst_ref=back.at[peer],
+            send_sem=row_send.at[0, 0],
+            recv_sem=row_recv.at[peer],
+            device_id=(peer // lanes, lax.rem(peer, lanes)),
+            device_id_type=MESH,
+        )
+
+    row_stay = pltpu.make_async_copy(row_grads.at[layer, my_seat], back.at[me], row_own)
+
+    def sum_copies(group, slot):
+        return [
+            pltpu.make_async_remote_copy(
+                src_ref=src.at[group],
+                dst_ref=dst.at[my_group],
+                send_sem=send.at[slot],
+                recv_sem=recv.at[slot],
+                device_id=(group, my_lane),
+                device_id_type=MESH,
+            )
+            for src, dst, send, recv in (
+                (part_in, got_in, in_send, in_recv),
+                (part_down, got_down, down_sent, down_recv),
+            )
+        ]
+
+    def pick(source, view):
+        facts = view[:, full - 128:].astype(F32).T
+        slots = lax.broadcasted_iota(jnp.int32, (batch, tok_count), 0).astype(F32)
+        here = layer.astype(F32)
+        first = ((facts[2:3] == here) & (facts[4:5] == slots)).astype(F32)
+        second = ((facts[3:4] == here) & (facts[5:6] == slots)).astype(F32)
+        chosen = (first + second).astype(BF16)
+        step = 1024
+        for begin in range(0, full - 128, step):
+            got = jnp.dot(chosen, view[:, begin:begin + step], preferred_element_type=F32)
+            picked[source, :, :, begin:begin + step] = got.astype(BF16).reshape(plane, cap, step)
+        weights = jnp.sum(first * facts[0:1] + second * facts[1:2], axis=1, keepdims=True)
+        tail = jnp.broadcast_to(weights, (batch, 128)).astype(BF16)
+        picked[source, :, :, full - 128:] = tail.reshape(plane, cap, 128)
+        own_copy(source).start()
+
+        @pl.loop(1, plane)
+        def _(off):
+            spread(source, off).start()
+
+    def work(source):
+        own_copy(source).wait()
+
+        @pl.loop(1, plane)
+        def _(off):
+            spread(source, off).wait_recv()
+
+        row_x = rows[source, :, :, :width].reshape(batch, width)
+        row_dy = rows[source, :, :, width:2 * width].reshape(batch, width)
+        weight = rows[source, :, :, 2 * width:].reshape(batch, 128)[:, :1].astype(F32)
+        both = jnp.dot(row_x, w_in[...], preferred_element_type=F32)
+        back_act = jnp.dot(row_dy, w_down[...], preferred_element_type=F32)
+        gate_pre = both[:, :hidden]
+        up_part = both[:, hidden:]
+        sig = jax.nn.sigmoid(gate_pre)
+        silu = gate_pre * sig
+        act = silu * up_part
+        gate_grad = jnp.sum(act * back_act, axis=1, keepdims=True)
+        act_grad = weight * back_act
+        gated[source] = (weight * act).astype(BF16)
+        gate_side = act_grad * up_part * sig * (1.0 + gate_pre * (1.0 - sig))
+        both_grads[source, :, :hidden] = gate_side.astype(BF16)
+        both_grads[source, :, hidden:] = (act_grad * silu).astype(BF16)
+        step = 512
+        for begin in range(0, width, step):
+            got = lax.dot_general(
+                both_grads[source], w_in[begin:begin + step, :], (((1,), (1,)), ((), ())),
+                preferred_element_type=F32)
+            row_grads[source, :, :, begin:begin + step] = got.astype(BF16).reshape(
+                plane, cap, step)
+        row_grads[source, :, :, width:] = jnp.broadcast_to(gate_grad, (batch, 128)).astype(
+            BF16).reshape(plane, cap, 128)
+
+        @pl.loop(0, plane)
+        def _(seat):
+            mine = (source == layer) & (seat == my_seat)
+
+            @pl.when(mine)
+            def _():
+                row_stay.start()
+
+            @pl.when(jnp.logical_not(mine))
+            def _():
+                row_copy(source, seat).start()
+
+    below_count = layer
+    above_count = outer - 1 - layer
+    paired = jnp.minimum(below_count, above_count)
+
+    def turn(q):
+        odd = lax.rem(q, 2)
+        in_pairs = (q <= 2 * paired).astype(jnp.int32)
+        far = in_pairs * ((q + 1) // 2) + (1 - in_pairs) * (q - paired)
+        longer = (below_count > above_count).astype(jnp.int32)
+        from_below = in_pairs * odd + (1 - in_pairs) * longer
+        return layer + far - 2 * far * from_below, from_below
+
+    for part in range(PIECES):
+        @pl.when(layer < outer - 1)
+        def _():
+            hop(layer, part, True, True).start()
+
+        @pl.when(layer > 0)
+        def _():
+            hop(layer, part, False, True).start()
+    pick(layer, tok_ref)
+    load_in.wait()
+    load_down.wait()
+
+    @pl.loop(1, outer + 1)
+    def _(q):
+        @pl.when(q < outer)
+        def _():
+            source, from_below = turn(q)
+            for part in range(PIECES):
+                hop(source, part, True, False).wait_recv()
+
+                @pl.when((from_below == 1) & (layer < outer - 1))
+                def _():
+                    hop(source, part, True, False).start()
+
+                @pl.when((from_below == 0) & (layer > 0))
+                def _():
+                    hop(source, part, False, False).start()
+            pick(source, held.at[source])
+
+        work(turn(q - 1)[0])
+
+    total = outer * batch
+    grads = both_grads[...].reshape(total, 2 * hidden)
+    acts = gated[...].reshape(total, hidden)
+
+    @pl.loop(0, groups)
+    def _(i):
+        off = lax.rem(i + groups // 2, groups)
+        group = lax.rem(my_group + off, groups)
+        columns = pl.ds(pl.multiple_of(group * share, share), share)
+        late = pl.ds(pl.multiple_of(width + group * share, share), share)
+        some_x = rows[:, :, :, columns].reshape(total, share)
+        part_in[group] = lax.dot_general(
+            some_x, grads, (((0,), (0,)), ((), ())), preferred_element_type=F32).astype(BF16)
+        some_dy = rows[:, :, :, late].reshape(total, share)
+        part_down[group] = lax.dot_general(
+            some_dy, acts, (((0,), (0,)), ((), ())), preferred_element_type=F32).astype(BF16)
+
+        @pl.when(off > 0)
+        def _():
+            for copy in sum_copies(group, off):
+                copy.start()
+
+    row_stay.wait()
+
+    @pl.loop(1, devices)
+    def _(off):
+        row_arrival(lax.rem(me + off, devices)).wait_recv()
+
+    places = lax.broadcasted_iota(jnp.int32, (tok_count, devices * cap), 1)
+    first = (slots_ref[:, 0:1] == places).astype(F32)
+    second = (slots_ref[:, 1:2] == places).astype(F32)
+    chosen = (first + second).astype(BF16)
+    for begin in range(0, width, 512):
+        view = back[:, :, begin:begin + 512].reshape(devices * cap, 512)
+        tokens_ref[:, begin:begin + 512] = jnp.dot(
+            chosen, view, preferred_element_type=F32).astype(BF16)
+    tail = back[:, :, width:].reshape(devices * cap, 128)
+    gate_first = jnp.dot(first.astype(BF16), tail, preferred_element_type=F32)
+    gate_second = jnp.dot(second.astype(BF16), tail, preferred_element_type=F32)
+    lane_ids = lax.broadcasted_iota(jnp.int32, (tok_count, 128), 1)
+    gates_ref[...] = jnp.where(lane_ids == 0, gate_first, gate_second).astype(BF16)
+
+    got_in[my_group] = part_in[my_group]
+    got_down[my_group] = part_down[my_group]
+    for off in range(1, groups):
+        for copy in sum_copies(lax.rem(my_group + off, groups), off):
+            copy.wait()
+
+    @pl.loop(0, share // 16)
+    def _(i):
+        at = pl.ds(pl.multiple_of(i * 16, 16), 16)
+        for got, out in ((got_in, grad_in_ref), (got_down, grad_down_ref)):
+            blocks = [got[group, at].astype(F32) for group in range(groups)]
+            for expert in range(KPC):
+                flags = [mask_ref[expert * groups + group:expert * groups + group + 1, :1]
+                         for group in range(groups)]
+                out[expert, at] = sum(
+                    flag * block for flag, block in zip(flags, blocks)).astype(BF16)
+
+    for source in range(outer):
+        @pl.loop(1, plane)
+        def _(off):
+            spread(source, off).wait_send()
+
+        @pl.loop(0, plane)
+        def _(seat):
+            @pl.when(jnp.logical_not((source == layer) & (seat == my_seat)))
+            def _():
+                row_copy(source, seat).wait_send()
+
+        for part in range(PIECES):
+            @pl.when((source <= layer) & (layer < outer - 1))
+            def _():
+                hop(source, part, True, False).wait_send()
+
+            @pl.when((source >= layer) & (layer > 0))
+            def _():
+                hop(source, part, False, False).wait_send()
 
 
 def expert_backward(rows_x, rows_dy, rows_gate, w_in, w_down):
@@ -37,7 +338,7 @@
     return (row_grad, gate_grad, part_in, part_down)
 
 
-def shards(tokens_in, grad_out, replica_of, gate_weights, placement, w_in_rep, w_down_rep):
+def plain_shards(tokens_in, grad_out, replica_of, gate_weights, placement, w_in_rep, w_down_rep):
     tok_count, model_width = tokens_in.shape
     top_count = replica_of.shape[1]
     group_count = lax.axis_size("grp")
@@ -138,6 +439,95 @@
     return (d_tokens, d_gates, summed_in.astype(jnp.bfloat16), summed_down.astype(jnp.bfloat16))
 
 
+def shards(tokens_in, grad_out, replica_of, gate_weights, placement, w_in_rep, w_down_rep):
+    tok_count, width = tokens_in.shape
+    top_count = replica_of.shape[1]
+    groups = lax.axis_size("grp")
+    lanes = lax.axis_size("ep")
+    devices = groups * lanes
+    cap = max(2, 2 * tok_count * top_count // devices)
+    if cap % 16 or top_count != 2:
+        return plain_shards(
+            tokens_in, grad_out, replica_of, gate_weights, placement, w_in_rep, w_down_rep
+        )
+    inner = max(1, min(lanes, tok_count // (groups * cap)))
+    outer = lanes // inner
+    plane = groups * inner
+    w_in = w_in_rep[0, 0]
+    w_down = w_down_rep[0, 0]
+    hidden = w_down.shape[1]
+    dest_rows = replica_of.reshape(-1)
+    row_ids = jnp.arange(tok_count * top_count, dtype=jnp.int32)
+    earlier = (dest_rows[:, None] == dest_rows[None, :]) & (row_ids[None, :] < row_ids[:, None])
+    rank_in = jnp.sum(earlier.astype(jnp.int32), axis=1).reshape(tok_count, top_count)
+    lane_of = replica_of % lanes
+    seat_of = replica_of // lanes * inner + lane_of % inner
+    facts = jnp.concatenate(
+        [
+            gate_weights,
+            (lane_of // inner).astype(BF16),
+            (seat_of * cap + rank_in).astype(BF16),
+            jnp.zeros((tok_count, 128 - 3 * top_count), BF16),
+        ],
+        axis=1,
+    )
+    tok = jnp.concatenate([tokens_in, grad_out, facts], axis=1)
+    full = tok.shape[1]
+    any_spec = pl.BlockSpec(memory_space=pl.ANY)
+    vmem_spec = pl.BlockSpec(memory_space=pltpu.VMEM)
+    dma = pltpu.SemaphoreType.DMA
+    share = width // groups
+    column = placement[:, lax.axis_index("ep")]
+    held_here = column[None, :] == jnp.arange(KPC, dtype=jnp.int32)[:, None]
+    mask = jnp.broadcast_to(held_here.astype(F32).reshape(KPC * groups, 1), (KPC * groups, 128))
+    batch = plane * cap
+    d_tokens, gates, grad_in, grad_down = pl.pallas_call(
+        functools.partial(layer_kernel, groups, lanes, inner, cap),
+        out_shape=(
+            jax.ShapeDtypeStruct((tok_count, width), BF16),
+            jax.ShapeDtypeStruct((tok_count, 128), BF16),
+            jax.ShapeDtypeStruct((KPC, share, 2 * hidden), BF16),
+            jax.ShapeDtypeStruct((KPC, share, hidden), BF16),
+        ),
+        in_specs=[vmem_spec, vmem_spec, vmem_spec, any_spec, any_spec],
+        out_specs=(vmem_spec,) * 4,
+        scratch_shapes=[
+            pltpu.VMEM((outer, tok_count, full), BF16),
+            pltpu.VMEM((outer, plane, cap, full), BF16),
+            pltpu.VMEM((outer, plane, cap, full), BF16),
+            pltpu.VMEM((width, 2 * hidden), BF16),
+            pltpu.VMEM((width, hidden), BF16),
+            pltpu.VMEM((outer, batch, 2 * hidden), BF16),
+            pltpu.VMEM((outer, batch, hidden), BF16),
+            pltpu.VMEM((outer, plane, cap, width + 128), BF16),
+            pltpu.VMEM((devices, cap, width + 128), BF16),
+            pltpu.VMEM((groups, share, 2 * hidden), BF16),
+            pltpu.VMEM((groups, share, hidden), BF16),
+            pltpu.VMEM((groups, share, 2 * hidden), BF16),
+            pltpu.VMEM((groups, share, hidden), BF16),
+            dma((outer, PIECES)),
+            dma((outer, PIECES)),
+            dma((outer, PIECES)),
+            dma((outer, plane)),
+            dma((outer, plane)),
+            dma((outer,)),
+            dma((2,)),
+            dma((outer, plane)),
+            dma((devices,)),
+            dma,
+            dma((groups,)),
+            dma((groups,)),
+            dma((groups,)),
+            dma((groups,)),
+        ],
+        compiler_params=pltpu.CompilerParams(
+            collective_id=0, has_side_effects=True, vmem_limit_bytes=58 * 2**20
+        ),
+        name="layer_backward",
+    )(tok, replica_of * cap + rank_in, mask, w_in, w_down)
+    return d_tokens, gates[:, :top_count], grad_in, grad_down
+
+
 def solution(mesh):
     placed = (
         P(("grp", "ep"), None),

time: 366 us -> 220 us (0.60)
  Pallas kernels: 0 us -> 202 us
  waiting for transfers between devices: 156 us -> 0 us
  blocking collectives: 53.3 us -> 0 us
  starting transfers between devices: 45.4 us -> 0 us
  matrix products: 27.9 us -> 0 us
  local copies, waits for them, and re-layouts: 38.8 us -> 14.1 us
  other arithmetic: 26.7 us -> 2.31 us
  between operations: 14.2 us -> 0.67 us
    pallas_call x0 -> x1, Pallas kernels: none -> 202 us  [shards(): pl.pallas_call(functools.partial(layer_kernel, groups, lanes, inner, cap)...]
    all_to_all x9 -> x0, waiting for transfers between devices: 156 us -> none  [the longest x1 44.8 us: shards(): lax.all_to_all(lax.all_to_all(returning[0], 'grp', split_axis=0, concat_a...]
    all_to_all x1 -> x0, blocking collectives: 53.3 us -> none  [shards(): lax.all_to_all(outgoing[0], 'ep', split_axis=1, concat_axis=1, tiled=True)]
    all_to_all x9 -> x0, starting transfers between devices: 45.1 us -> none  [the longest x1 5.88 us: shards(): lax.all_to_all(lax.all_to_all(outgoing[0], 'ep', split_axis=1, concat_axi...]
    dot_general x6 -> x0, matrix products: 27.9 us -> none  [the longest x1 8.05 us: expert_backward(): lax.dot_general(rows_x, both_grad, (((0,), (0,)), ((), ())), preferred_el...]
    gather x5 -> x0, local copies, waits for them, and re-layouts: 16.1 us -> none  [the longest x1 4.22 us: shards(): came_back[0].reshape(device_count * capacity, model_width)[send_slot]]
    convert_element_type x6 -> x2, other arithmetic: 16.6 us -> 0.76 us  [the longest x1 0.75 us: shards(): (seat_of * cap + rank_in).astype(BF16)]
    all_to_all x7 -> x0, local copies, waits for them, and re-layouts: 13.9 us -> none  [the longest x1 3.19 us: shards(): lax.all_to_all(outgoing[1], 'ep', split_axis=1, concat_axis=1, tiled=True)]
  transfers between devices with their start and end apart: 11 -> 0, of which waited for: 6 -> 0; matrix products, arithmetic and copies ran while one was open for 20% -> 0% of each run, Pallas kernels for 0% -> 0%
where the time goes in v2:
time: 220 us; the launch traced here: 219 us
  Pallas kernels  202 us (92%)
  local copies, waits for them, and re-layouts  14.1 us (6%)
  other arithmetic  2.31 us (1%)
    pallas_call x1, Pallas kernels, shards(): pl.pallas_call(functools.partial(layer_kernel, groups, lanes, inner, cap)...  202 us
    unnamed x10, local copies, waits for them, and re-layouts  9.62 us

profile of v2, /device:TPU:5, one launch (start us, length us, event | category | flops | bytes accessed | tf_op | source)
XLA Modules:
  0.0 219.0 jit_solution(18023349103265131778)
XLA Ops:
  0.6 0.0 copy-start
  0.6 0.7 copy-done
  1.3 0.2 dynamic-slice_reduce_fusion
  1.5 0.1 reshape.33
  1.6 0.7 broadcast_compare_fusion
  2.3 0.7 broadcast_multiply_fusion
  3.0 0.7 broadcast_in_dim.5.mask_ref
  3.6 0.1 copy.38
  3.8 0.8 copy.42
  4.5 0.1 copy.44
  4.7 0.8 copy.35
  5.4 0.1 eq.38
  5.6 0.2 convert_reduce_fusion
  5.8 0.1 reshape.32
  5.9 0.8 fusion.6
  6.7 3.1 %concatenate.3.tok_ref = bf16[128,4224]{1,0:T(8,128)(2,1)} concatenate(bf16[128,2048]{1,0:T(8,128)(2,1)} %param.7, bf16[128,2048]{1,0:T(8,128)(2,1)} %param.8, bf16[128,2]{1,0:T(8,128)(2,1)S(1)} %copy.42, bf16[128,2]{1,0:T(8,128)(2,1)S(1)} %get-tuple-element.25, bf16[128,2]{1,0:T(8,128)(2,1)S(1)} %get-tuple-element.24, bf16[128,122]{1,0:T(8,128)(2,1)S(1)} %broadcast_in_dim.4), dimensions={1} | concatenate | bytes 2162688 | tf_op jit(solution)/shard_map/concatenate | solution.py:474
  9.7 201.9 %layer_backward.1 = (bf16[128,2048]{1,0:T(8,128)(2,1)}, bf16[128,128]{1,0:T(8,128)(2,1)}, bf16[2,512,1024]{2,1,0:T(8,128)(2,1)}, bf16[2,512,512]{2,1,0:T(8,128)(2,1)}) custom-call(bf16[128,4224]{1,0:T(8,128)(2,1)} %concatenate.3.tok_ref, s32[128,2]{1,0:T(8,128)} %get-tuple-element.26.slots_ref, f32[8,128]{1,0:T(8,128)} %broadcast_in_dim.5.mask_ref, ...), custom_call_target="tpu_custom_call" | custom-call | tf_op jit(solution)/shard_map/layer_backward/pallas_call | solution.py:484
  211.6 1.4 copy.45
  213.0 1.9 copy.52
  214.9 0.0 copy-start.1
  214.9 3.2 %copy.53 = bf16[2,512,1024]{2,1,0:T(8,128)(2,1)} copy(bf16[2,512,1024]{2,1,0:T(8,128)(2,1)} %get-tuple-element.33) | data formatting | bytes 4194304
  218.0 0.0 copy-done.1
  218.0 1.0 copy.54
  (2 shorter events, 0.0 us)
Async XLA Ops:
  0.6 0.7 copy-start
  214.9 3.2 %copy-start.1 = (bf16[2,512,512]{2,1,0:T(8,128)(2,1)S(1)}, bf16[2,512,512]{2,1,0:T(8,128)(2,1)}, u32[]{:S(2)}) copy-start(bf16[2,512,512]{2,1,0:T(8,128)(2,1)} %get-tuple-element.34) | copy-start | bytes 3145732

commit v3 on v2

--- a/solution.py
+++ b/solution.py
@@ -16,23 +16,31 @@
 
 def layer_kernel(groups, lanes, inner, cap, tok_ref, slots_ref, mask_ref, w_in_hbm, w_down_hbm,
                  tokens_ref, gates_ref, grad_in_ref, grad_down_ref,
-                 held, picked, rows, w_in, w_down, both_grads, gated, row_grads, back,
-                 part_in, part_down, got_in, got_down,
+                 held, picked, rows, w_in, w_down, other_in, other_down,
+                 both_grads, gated, row_grads, back,
+                 sib_in, sib_down, from_in, from_down, cross_in, cross_down, got_in, got_down,
                  up_send, down_send, chain_recv, plane_send, plane_recv, own_sem, load_sem,
-                 row_send, row_recv, row_own, in_send, in_recv, down_sent, down_recv):
+                 row_send, row_recv, row_own, swap_send, swap_recv, sib_send, sib_recv,
+                 cross_send, cross_recv):
     tok_count, full = tok_ref.shape
     width = (full - 128) // 2
     hidden = w_down.shape[1]
     outer = lanes // inner
-    plane = groups * inner
+    plane = groups // 2 * inner
     devices = groups * lanes
     batch = plane * cap
+    senders = groups // 2 * lanes
     share = width // groups
     my_group = lax.axis_index("grp")
     my_lane = lax.axis_index("ep")
     me = my_group * lanes + my_lane
     layer = my_lane // inner
-    my_seat = my_group * inner + lax.rem(my_lane, inner)
+    side = my_group // 2
+    core = lax.rem(my_group, 2)
+    my_seat = side * inner + lax.rem(my_lane, inner)
+    my_sender = side * lanes + my_lane
+    sibling = (side * 2 + 1 - core, my_lane)
+    across = ((1 - side) * 2 + core, my_lane)
     step_rows = tok_count // PIECES
 
     load_in = pltpu.make_async_copy(w_in_hbm, w_in, load_sem.at[0])
@@ -49,6 +57,18 @@
                             device_id_type=MESH)
 
     pl.semaphore_wait(barrier, devices - 1)
+
+    def remote(src, dst, send, recv, device):
+        return pltpu.make_async_remote_copy(
+            src_ref=src, dst_ref=dst, send_sem=send, recv_sem=recv,
+            device_id=device, device_id_type=MESH)
+
+    swaps = [
+        remote(w_in_hbm, other_in, swap_send.at[0], swap_recv.at[0], sibling),
+        remote(w_down_hbm, other_down, swap_send.at[1], swap_recv.at[1], sibling),
+    ]
+    for swap in swaps:
+        swap.start()
 
     def piece(source, part):
         return held.at[source, pl.ds(part * step_rows, step_rows)]
@@ -72,7 +92,7 @@
             dst_ref=rows.at[source, my_seat],
             send_sem=plane_send.at[source, off],
             recv_sem=plane_recv.at[source, off],
-            device_id=(seat // inner, layer * inner + lax.rem(seat, inner)),
+            device_id=(seat // inner * 2 + core, layer * inner + lax.rem(seat, inner)),
             device_id_type=MESH,
         )
 
@@ -84,10 +104,10 @@
     def row_copy(source, seat):
         return pltpu.make_async_remote_copy(
             src_ref=row_grads.at[source, seat],
-            dst_ref=back.at[me],
+            dst_ref=back.at[my_sender],
             send_sem=row_send.at[source, seat],
-            recv_sem=row_recv.at[me],
-            device_id=(seat // inner, source * inner + lax.rem(seat, inner)),
+            recv_sem=row_recv.at[my_sender],
+            device_id=(seat // inner * 2 + core, source * inner + lax.rem(seat, inner)),
             device_id_type=MESH,
         )
 
@@ -97,27 +117,11 @@
             dst_ref=back.at[peer],
             send_sem=row_send.at[0, 0],
             recv_sem=row_recv.at[peer],
-            device_id=(peer // lanes, lax.rem(peer, lanes)),
+            device_id=(peer // lanes * 2 + core, lax.rem(peer, lanes)),
             device_id_type=MESH,
         )
 
-    row_stay = pltpu.make_async_copy(row_grads.at[layer, my_seat], back.at[me], row_own)
-
-    def sum_copies(group, slot):
-        return [
-            pltpu.make_async_remote_copy(
-                src_ref=src.at[group],
-                dst_ref=dst.at[my_group],
-                send_sem=send.at[slot],
-                recv_sem=recv.at[slot],
-                device_id=(group, my_lane),
-                device_id_type=MESH,
-            )
-            for src, dst, send, recv in (
-                (part_in, got_in, in_send, in_recv),
-                (part_down, got_down, down_sent, down_recv),
-            )
-        ]
+    row_stay = pltpu.make_async_copy(row_grads.at[layer, my_seat], back.at[my_sender], row_own)
 
     def pick(source, view):
         facts = view[:, full - 128:].astype(F32).T
@@ -207,6 +211,16 @@
     pick(layer, tok_ref)
     load_in.wait()
     load_down.wait()
+    for swap in swaps:
+        swap.wait()
+
+    @pl.loop(0, width // 64)
+    def _(i):
+        at = pl.ds(pl.multiple_of(i * 64, 64), 64)
+        mine = mask_ref[0:1, :1].astype(BF16)
+        theirs = mask_ref[1:2, :1].astype(BF16)
+        w_in[at] = mine * w_in[at] + theirs * other_in[at]
+        w_down[at] = mine * w_down[at] + theirs * other_down[at]
 
     @pl.loop(1, outer + 1)
     def _(q):
@@ -231,60 +245,76 @@
     grads = both_grads[...].reshape(total, 2 * hidden)
     acts = gated[...].reshape(total, hidden)
 
-    @pl.loop(0, groups)
-    def _(i):
-        off = lax.rem(i + groups // 2, groups)
-        group = lax.rem(my_group + off, groups)
-        columns = pl.ds(pl.multiple_of(group * share, share), share)
-        late = pl.ds(pl.multiple_of(width + group * share, share), share)
-        some_x = rows[:, :, :, columns].reshape(total, share)
-        part_in[group] = lax.dot_general(
-            some_x, grads, (((0,), (0,)), ((), ())), preferred_element_type=F32).astype(BF16)
-        some_dy = rows[:, :, :, late].reshape(total, share)
-        part_down[group] = lax.dot_general(
-            some_dy, acts, (((0,), (0,)), ((), ())), preferred_element_type=F32).astype(BF16)
-
-        @pl.when(off > 0)
-        def _():
-            for copy in sum_copies(group, off):
-                copy.start()
+    def part_of(group, begin, other):
+        columns = pl.ds(pl.multiple_of(begin + group * share, share), share)
+        some = rows[:, :, :, columns].reshape(total, share)
+        return lax.dot_general(some, other, (((0,), (0,)), ((), ())), preferred_element_type=F32)
+
+    kinds = (
+        (0, grads, sib_in, from_in, cross_in, got_in, grad_in_ref),
+        (width, acts, sib_down, from_down, cross_down, got_down, grad_down_ref),
+    )
+
+    def to_sibling(kind, which):
+        return remote(kinds[kind][2].at[which], kinds[kind][3].at[which],
+                      sib_send.at[kind, which], sib_recv.at[kind, which], sibling)
+
+    def to_across(kind):
+        return remote(kinds[kind][4], kinds[kind][5], cross_send.at[kind], cross_recv.at[kind],
+                      across)
+
+    for which, target in ((0, 1 - side), (1, side)):
+        for kind in range(2):
+            begin, other, sib = kinds[kind][:3]
+            sib[which] = part_of(target * 2 + 1 - core, begin, other).astype(BF16)
+            to_sibling(kind, which).start()
+        for kind in range(2):
+            begin, other, _, arrived, crossing, _, out = kinds[kind]
+            mine = part_of(target * 2 + core, begin, other)
+            to_sibling(kind, which).wait_recv()
+            joined = (mine + arrived[which].astype(F32)).astype(BF16)
+            if which == 0:
+                crossing[...] = joined
+                to_across(kind).start()
+            else:
+                out[0] = joined
 
     row_stay.wait()
 
-    @pl.loop(1, devices)
+    @pl.loop(1, senders)
     def _(off):
-        row_arrival(lax.rem(me + off, devices)).wait_recv()
-
-    places = lax.broadcasted_iota(jnp.int32, (tok_count, devices * cap), 1)
+        row_arrival(lax.rem(my_sender + off, senders)).wait_recv()
+
+    places = lax.broadcasted_iota(jnp.int32, (tok_count, senders * cap), 1)
     first = (slots_ref[:, 0:1] == places).astype(F32)
     second = (slots_ref[:, 1:2] == places).astype(F32)
     chosen = (first + second).astype(BF16)
     for begin in range(0, width, 512):
-        view = back[:, :, begin:begin + 512].reshape(devices * cap, 512)
+        view = back[:, :, begin:begin + 512].reshape(senders * cap, 512)
         tokens_ref[:, begin:begin + 512] = jnp.dot(
             chosen, view, preferred_element_type=F32).astype(BF16)
-    tail = back[:, :, width:].reshape(devices * cap, 128)
+    tail = back[:, :, width:].reshape(senders * cap, 128)
     gate_first = jnp.dot(first.astype(BF16), tail, preferred_element_type=F32)
     gate_second = jnp.dot(second.astype(BF16), tail, preferred_element_type=F32)
     lane_ids = lax.broadcasted_iota(jnp.int32, (tok_count, 128), 1)
     gates_ref[...] = jnp.where(lane_ids == 0, gate_first, gate_second).astype(BF16)
 
-    got_in[my_group] = part_in[my_group]
-    got_down[my_group] = part_down[my_group]
-    for off in range(1, groups):
-        for copy in sum_copies(lax.rem(my_group + off, groups), off):
-            copy.wait()
+    for kind in range(2):
+        to_across(kind).wait()
+        to_sibling(kind, 0).wait_send()
+        to_sibling(kind, 1).wait_send()
 
     @pl.loop(0, share // 16)
     def _(i):
         at = pl.ds(pl.multiple_of(i * 16, 16), 16)
-        for got, out in ((got_in, grad_in_ref), (got_down, grad_down_ref)):
-            blocks = [got[group, at].astype(F32) for group in range(groups)]
-            for expert in range(KPC):
-                flags = [mask_ref[expert * groups + group:expert * groups + group + 1, :1]
-                         for group in range(groups)]
-                out[expert, at] = sum(
-                    flag * block for flag, block in zip(flags, blocks)).astype(BF16)
+        for kind in range(2):
+            got, out = kinds[kind][5:]
+            near = out[0, at].astype(F32)
+            away = got[at].astype(F32)
+            lower = mask_ref[2:3, :1]
+            upper = mask_ref[3:4, :1]
+            out[0, at] = (lower * near + upper * away).astype(BF16)
+            out[1, at] = (upper * near + lower * away).astype(BF16)
 
     for source in range(outer):
         @pl.loop(1, plane)
@@ -446,13 +476,14 @@
     lanes = lax.axis_size("ep")
     devices = groups * lanes
     cap = max(2, 2 * tok_count * top_count // devices)
-    if cap % 16 or top_count != 2:
+    if cap % 16 or top_count != 2 or groups != 4:
         return plain_shards(
             tokens_in, grad_out, replica_of, gate_weights, placement, w_in_rep, w_down_rep
         )
     inner = max(1, min(lanes, tok_count // (groups * cap)))
     outer = lanes // inner
-    plane = groups * inner
+    plane = groups // 2 * inner
+    senders = groups // 2 * lanes
     w_in = w_in_rep[0, 0]
     w_down = w_down_rep[0, 0]
     hidden = w_down.shape[1]
@@ -460,13 +491,25 @@
     row_ids = jnp.arange(tok_count * top_count, dtype=jnp.int32)
     earlier = (dest_rows[:, None] == dest_rows[None, :]) & (row_ids[None, :] < row_ids[:, None])
     rank_in = jnp.sum(earlier.astype(jnp.int32), axis=1).reshape(tok_count, top_count)
+    first_fits = (placement[2] != placement[0]) | (placement[3] != placement[0])
+    low_expert = jnp.where(first_fits, placement[0], placement[1])
+    side_table = jnp.where(placement == low_expert[None, :], 0, 1)
+    same = placement[:, None, :] == placement[None, :, :]
+    before = jnp.arange(groups)[None, :, None] < jnp.arange(groups)[:, None, None]
+    copy_table = jnp.sum((same & before).astype(jnp.int32), axis=1)
+    table = (side_table * groups + copy_table).reshape(-1)
+    named = replica_of[:, :, None] == jnp.arange(devices, dtype=jnp.int32)
+    entry = jnp.sum(jnp.where(named, table, 0), axis=2)
+    side_of = entry // groups
+    spot = entry % groups * cap + rank_in
+    cap = (groups - 1) * cap
     lane_of = replica_of % lanes
-    seat_of = replica_of // lanes * inner + lane_of % inner
+    seat_of = side_of * inner + lane_of % inner
     facts = jnp.concatenate(
         [
             gate_weights,
             (lane_of // inner).astype(BF16),
-            (seat_of * cap + rank_in).astype(BF16),
+            (seat_of * cap + spot).astype(BF16),
             jnp.zeros((tok_count, 128 - 3 * top_count), BF16),
         ],
         axis=1,
@@ -477,9 +520,13 @@
     vmem_spec = pl.BlockSpec(memory_space=pltpu.VMEM)
     dma = pltpu.SemaphoreType.DMA
     share = width // groups
-    column = placement[:, lax.axis_index("ep")]
-    held_here = column[None, :] == jnp.arange(KPC, dtype=jnp.int32)[:, None]
-    mask = jnp.broadcast_to(held_here.astype(F32).reshape(KPC * groups, 1), (KPC * groups, 128))
+    my_group = lax.axis_index("grp")
+    my_lane = lax.axis_index("ep")
+    side = my_group // 2
+    my_expert = jnp.where(side == 0, low_expert[my_lane], 1 - low_expert[my_lane])
+    own_fits = placement[my_group, my_lane] == my_expert
+    choices = jnp.stack([own_fits, ~own_fits, my_expert == 0, my_expert == 1]).astype(F32)
+    mask = jnp.broadcast_to(jnp.pad(choices, (0, 4))[:, None], (8, 128))
     batch = plane * cap
     d_tokens, gates, grad_in, grad_down = pl.pallas_call(
         functools.partial(layer_kernel, groups, lanes, inner, cap),
@@ -497,14 +544,20 @@
             pltpu.VMEM((outer, plane, cap, full), BF16),
             pltpu.VMEM((width, 2 * hidden), BF16),
             pltpu.VMEM((width, hidden), BF16),
+            pltpu.VMEM((width, 2 * hidden), BF16),
+            pltpu.VMEM((width, hidden), BF16),
             pltpu.VMEM((outer, batch, 2 * hidden), BF16),
             pltpu.VMEM((outer, batch, hidden), BF16),
             pltpu.VMEM((outer, plane, cap, width + 128), BF16),
-            pltpu.VMEM((devices, cap, width + 128), BF16),
-            pltpu.VMEM((groups, share, 2 * hidden), BF16),
-            pltpu.VMEM((groups, share, hidden), BF16),
-            pltpu.VMEM((groups, share, 2 * hidden), BF16),
-            pltpu.VMEM((groups, share, hidden), BF16),
+            pltpu.VMEM((senders, cap, width + 128), BF16),
+            pltpu.VMEM((2, share, 2 * hidden), BF16),
+            pltpu.VMEM((2, share, hidden), BF16),
+            pltpu.VMEM((2, share, 2 * hidden), BF16),
+            pltpu.VMEM((2, share, hidden), BF16),
+            pltpu.VMEM((share, 2 * hidden), BF16),
+            pltpu.VMEM((share, hidden), BF16),
+            pltpu.VMEM((share, 2 * hidden), BF16),
+            pltpu.VMEM((share, hidden), BF16),
             dma((outer, PIECES)),
             dma((outer, PIECES)),
             dma((outer, PIECES)),
@@ -513,18 +566,20 @@
             dma((outer,)),
             dma((2,)),
             dma((outer, plane)),
-            dma((devices,)),
+            dma((senders,)),
             dma,
-            dma((groups,)),
-            dma((groups,)),
-            dma((groups,)),
-            dma((groups,)),
+            dma((2,)),
+            dma((2,)),
+            dma((2, 2)),
+            dma((2, 2)),
+            dma((2,)),
+            dma((2,)),
         ],
         compiler_params=pltpu.CompilerParams(
             collective_id=0, has_side_effects=True, vmem_limit_bytes=58 * 2**20
         ),
         name="layer_backward",
-    )(tok, replica_of * cap + rank_in, mask, w_in, w_down)
+    )(tok, (side_of * lanes + lane_of) * cap + spot, mask, w_in, w_down)
     return d_tokens, gates[:, :top_count], grad_in, grad_down
 
 

time: 220 us -> 217 us (0.986)
  Pallas kernels: 202 us -> 193 us
  other arithmetic: 2.31 us -> 5.72 us
    pallas_call x1, Pallas kernels: 202 us -> 193 us  [shards(): pl.pallas_call(functools.partial(layer_kernel, groups, lanes, inner, cap)...]
    unnamed x10 -> x8, local copies, waits for them, and re-layouts: 9.62 us -> 8.94 us
where the time goes in v3:
time: 217 us; the launch traced here: 216 us
  Pallas kernels  193 us (89%)
  local copies, waits for them, and re-layouts  15.1 us (7%)
  other arithmetic  5.72 us (3%)
  between operations  2.63 us (1%)
    pallas_call x1, Pallas kernels, shards(): pl.pallas_call(functools.partial(layer_kernel, groups, lanes, inner, cap)...  193 us
    unnamed x8, local copies, waits for them, and re-layouts  8.94 us

profile of v3, /device:TPU:5, one launch (start us, length us, event | category | flops | bytes accessed | tf_op | source)
XLA Modules:
  0.0 216.4 jit_solution(18149814716165636554)
XLA Ops:
  0.6 1.3 dynamic_slice.7
  1.9 0.7 broadcast_compare_fusion
  2.6 0.8 or_select_fusion
  3.4 0.6 dynamic_slice.8
  6.1 0.8 fusion.13
  6.9 0.8 convert_reduce_fusion.1
  7.7 0.7 multiply_add_fusion.1
  8.4 0.1 reshape.35
  8.5 0.8 select_reduce_fusion
  9.3 0.7 broadcast_in_dim.39.mask_ref
  9.9 0.1 copy.32
  10.1 0.8 copy.38
  10.9 0.1 copy.33
  11.0 0.8 copy.29
  11.8 0.1 eq.76
  11.9 0.2 convert_reduce_fusion
  12.1 0.1 reshape.36
  12.2 0.8 multiply_add_fusion
  13.0 3.1 %concatenate.3.tok_ref = bf16[128,4224]{1,0:T(8,128)(2,1)} concatenate(bf16[128,2048]{1,0:T(8,128)(2,1)} %param.7, bf16[128,2048]{1,0:T(8,128)(2,1)} %param.8, bf16[128,2]{1,0:T(8,128)(2,1)S(1)} %copy.38, bf16[128,2]{1,0:T(8,128)(2,1)S(1)} %get-tuple-element.26, bf16[128,2]{1,0:T(8,128)(2,1)S(1)} %get-tuple-element.25, bf16[128,122]{1,0:T(8,128)(2,1)S(1)} %broadcast_in_dim.38), dimensions={1} | concatenate | bytes 2162688 | tf_op jit(solution)/shard_map/concatenate | solution.py:517
  16.1 193.0 %layer_backward.1 = (bf16[128,2048]{1,0:T(8,128)(2,1)}, bf16[128,128]{1,0:T(8,128)(2,1)}, bf16[2,512,1024]{2,1,0:T(8,128)(2,1)}, bf16[2,512,512]{2,1,0:T(8,128)(2,1)}) custom-call(bf16[128,4224]{1,0:T(8,128)(2,1)} %concatenate.3.tok_ref, s32[128,2]{1,0:T(8,128)} %get-tuple-element.24.slots_ref, f32[8,128]{1,0:T(8,128)} %broadcast_in_dim.39.mask_ref, ...), custom_call_target="tpu_custom_call" | custom-call | tf_op jit(solution)/shard_map/layer_backward/pallas_call | solution.py:531
  209.1 1.4 copy.39
  210.4 1.9 copy.51
  212.3 3.2 %copy.52 = bf16[2,512,1024]{2,1,0:T(8,128)(2,1)} copy(bf16[2,512,1024]{2,1,0:T(8,128)(2,1)} %get-tuple-element.33) | data formatting | bytes 4194304
  215.5 1.0 copy.53
  (6 shorter events, 0.1 us)
Async XLA Ops:
  212.3 3.2 %copy-start = (bf16[2,512,512]{2,1,0:T(8,128)(2,1)S(1)}, bf16[2,512,512]{2,1,0:T(8,128)(2,1)}, u32[]{:S(2)}) copy-start(bf16[2,512,512]{2,1,0:T(8,128)(2,1)} %get-tuple-element.34) | copy-start | bytes 3145732

commit v4 on v3

--- a/solution.py
+++ b/solution.py
@@ -11,19 +11,23 @@
 MESH = pl.DeviceIdType.MESH
 F32 = jnp.float32
 BF16 = jnp.bfloat16
-PIECES = 4
-
-
-def layer_kernel(groups, lanes, inner, cap, tok_ref, slots_ref, mask_ref, w_in_hbm, w_down_hbm,
+PIECES = 5
+
+
+def layer_kernel(groups, lanes, inner, cap, x_ref, dy_ref, routes_ref, copies_ref,
+                 w_in_hbm, w_down_hbm,
                  tokens_ref, gates_ref, grad_in_ref, grad_down_ref,
-                 held, picked, rows, w_in, w_down, other_in, other_down,
+                 held_facts, held_x, held_dy, picked_x, picked_dy, rows_x, rows_dy, marks, flags,
+                 w_in, w_down, other_in, other_down,
                  both_grads, gated, row_grads, back,
                  sib_in, sib_down, from_in, from_down, cross_in, cross_down, got_in, got_down,
                  up_send, down_send, chain_recv, plane_send, plane_recv, own_sem, load_sem,
                  row_send, row_recv, row_own, swap_send, swap_recv, sib_send, sib_recv,
                  cross_send, cross_recv):
-    tok_count, full = tok_ref.shape
-    width = (full - 128) // 2
+    tok_count, width = x_ref.shape
+    full = width + 128
+    rows_each = cap
+    cap = (groups - 1) * cap
     hidden = w_down.shape[1]
     outer = lanes // inner
     plane = groups // 2 * inner
@@ -41,7 +45,7 @@
     my_sender = side * lanes + my_lane
     sibling = (side * 2 + 1 - core, my_lane)
     across = ((1 - side) * 2 + core, my_lane)
-    step_rows = tok_count // PIECES
+    half = tok_count // 2
 
     load_in = pltpu.make_async_copy(w_in_hbm, w_in, load_sem.at[0])
     load_down = pltpu.make_async_copy(w_down_hbm, w_down, load_sem.at[1])
@@ -70,36 +74,78 @@
     for swap in swaps:
         swap.start()
 
-    def piece(source, part):
-        return held.at[source, pl.ds(part * step_rows, step_rows)]
+    device_ids = lax.broadcasted_iota(jnp.int32, (1, 128), 1)
+    group_ids = device_ids // lanes
+    lane_in = device_ids - group_ids * lanes
+    copies = [copies_ref[group:group + 1] for group in range(groups)]
+    low = jnp.where((copies[2] != copies[0]) | (copies[3] != copies[0]), copies[0], copies[1])
+    mine = sum(jnp.where(group_ids == group, copies[group], 0.0) for group in range(groups))
+    side_table = (mine != low).astype(F32)
+    copy_table = sum(
+        ((copies[group] == mine) & (group_ids > group)).astype(F32) for group in range(groups))
+    layer_table = (lane_in // inner).astype(F32)
+    within_table = lax.rem(lane_in, inner).astype(F32)
+    copy_base = copy_table * rows_each
+    place_table = (side_table * inner + within_table) * cap + copy_base
+    back_table = (side_table * lanes + lane_in.astype(F32)) * cap + copy_base
+    here_only = device_ids == me
+    my_low = jnp.sum(jnp.where(here_only, low, 0.0), axis=1, keepdims=True)
+    my_held = jnp.sum(jnp.where(here_only, mine, 0.0), axis=1, keepdims=True)
+    on_high = side.astype(F32)
+    my_expert = my_low * (1.0 - on_high) + (1.0 - my_low) * on_high
+    flags[0:1] = jnp.broadcast_to((my_held == my_expert).astype(F32), (1, 128))
+    flags[1:2] = jnp.broadcast_to((my_held != my_expert).astype(F32), (1, 128))
+    flags[2:3] = jnp.broadcast_to(1.0 - my_expert, (1, 128))
+    flags[3:4] = jnp.broadcast_to(my_expert, (1, 128))
+    routes = routes_ref[...]
+    across_tokens = routes.T
+    token_ids = lax.broadcasted_iota(jnp.int32, (tok_count, tok_count), 0)
+    other_ids = lax.broadcasted_iota(jnp.int32, (tok_count, tok_count), 1)
+    earlier = other_ids < token_ids
+    column_ids = lax.broadcasted_iota(jnp.int32, (tok_count, 128), 1)
+    spread_ids = column_ids.astype(F32)
+    facts = jnp.where(column_ids < 2, pltpu.roll(routes, 126, 1), 0.0)
+    backs = jnp.zeros((tok_count, 128), F32)
+    for k in range(2):
+        named = routes[:, k:k + 1]
+        same = (named == across_tokens[0:1]).astype(F32) + (named == across_tokens[1:2]).astype(F32)
+        rank = jnp.sum(jnp.where(earlier, same, 0.0), axis=1, keepdims=True)
+        chosen = named == spread_ids
+
+        def look(table):
+            return jnp.sum(jnp.where(chosen, table, 0.0), axis=1, keepdims=True)
+
+        facts = jnp.where(column_ids == 2 + k, look(layer_table), facts)
+        facts = jnp.where(column_ids == 4 + k, look(place_table) + rank, facts)
+        backs = jnp.where(column_ids == k, look(back_table) + rank, backs)
+    held_facts[layer] = facts.astype(BF16)
+    marks[...] = backs
 
     def hop(source, part, upward, own):
-        src = tok_ref.at[pl.ds(part * step_rows, step_rows)] if own else piece(source, part)
+        if part == 0:
+            src = dst = held_facts.at[source]
+        else:
+            box, given = (held_x, x_ref) if part < 3 else (held_dy, dy_ref)
+            at = pl.ds((part - 1) % 2 * half, half)
+            dst = box.at[source, at]
+            src = given.at[at] if own else dst
         sems = up_send if upward else down_send
-        return pltpu.make_async_remote_copy(
-            src_ref=src,
-            dst_ref=piece(source, part),
-            send_sem=sems.at[source, part],
-            recv_sem=chain_recv.at[source, part],
-            device_id=(my_group, my_lane + inner if upward else my_lane - inner),
-            device_id_type=MESH,
-        )
-
-    def spread(source, off):
+        return remote(src, dst, sems.at[source, part], chain_recv.at[source, part],
+                      (my_group, my_lane + inner if upward else my_lane - inner))
+
+    boxes = ((picked_x, rows_x), (picked_dy, rows_dy))
+
+    def spread(source, off, kind):
         seat = lax.rem(my_seat + off, plane)
-        return pltpu.make_async_remote_copy(
-            src_ref=picked.at[source, seat],
-            dst_ref=rows.at[source, my_seat],
-            send_sem=plane_send.at[source, off],
-            recv_sem=plane_recv.at[source, off],
-            device_id=(seat // inner * 2 + core, layer * inner + lax.rem(seat, inner)),
-            device_id_type=MESH,
-        )
-
-    def own_copy(source):
+        src, dst = boxes[kind]
+        return remote(src.at[source, seat], dst.at[source, my_seat],
+                      plane_send.at[kind, source, off], plane_recv.at[kind, source, off],
+                      (seat // inner * 2 + core, layer * inner + lax.rem(seat, inner)))
+
+    def own_copy(source, kind):
+        src, dst = boxes[kind]
         return pltpu.make_async_copy(
-            picked.at[source, my_seat], rows.at[source, my_seat], own_sem.at[source]
-        )
+            src.at[source, my_seat], dst.at[source, my_seat], own_sem.at[kind, source])
 
     def row_copy(source, seat):
         return pltpu.make_async_remote_copy(
@@ -123,37 +169,42 @@
 
     row_stay = pltpu.make_async_copy(row_grads.at[layer, my_seat], back.at[my_sender], row_own)
 
-    def pick(source, view):
-        facts = view[:, full - 128:].astype(F32).T
+    def pick(source, view, kind):
+        facts = held_facts[source].astype(F32).T
         slots = lax.broadcasted_iota(jnp.int32, (batch, tok_count), 0).astype(F32)
         here = layer.astype(F32)
         first = ((facts[2:3] == here) & (facts[4:5] == slots)).astype(F32)
         second = ((facts[3:4] == here) & (facts[5:6] == slots)).astype(F32)
         chosen = (first + second).astype(BF16)
         step = 1024
-        for begin in range(0, full - 128, step):
+        picked = boxes[kind][0]
+        for begin in range(0, width, step):
             got = jnp.dot(chosen, view[:, begin:begin + step], preferred_element_type=F32)
             picked[source, :, :, begin:begin + step] = got.astype(BF16).reshape(plane, cap, step)
-        weights = jnp.sum(first * facts[0:1] + second * facts[1:2], axis=1, keepdims=True)
-        tail = jnp.broadcast_to(weights, (batch, 128)).astype(BF16)
-        picked[source, :, :, full - 128:] = tail.reshape(plane, cap, 128)
-        own_copy(source).start()
+        if kind == 0:
+            weights = jnp.sum(first * facts[0:1] + second * facts[1:2], axis=1, keepdims=True)
+            tail = jnp.broadcast_to(weights, (batch, 128)).astype(BF16)
+            picked[source, :, :, width:] = tail.reshape(plane, cap, 128)
+        own_copy(source, kind).start()
 
         @pl.loop(1, plane)
         def _(off):
-            spread(source, off).start()
-
-    def work(source):
-        own_copy(source).wait()
+            spread(source, off, kind).start()
+
+    def arrive(source, kind):
+        own_copy(source, kind).wait()
 
         @pl.loop(1, plane)
         def _(off):
-            spread(source, off).wait_recv()
-
-        row_x = rows[source, :, :, :width].reshape(batch, width)
-        row_dy = rows[source, :, :, width:2 * width].reshape(batch, width)
-        weight = rows[source, :, :, 2 * width:].reshape(batch, 128)[:, :1].astype(F32)
+            spread(source, off, kind).wait_recv()
+
+    def work(source):
+        arrive(source, 0)
+        row_x = rows_x[source, :, :, :width].reshape(batch, width)
+        weight = rows_x[source, :, :, width:].reshape(batch, 128)[:, :1].astype(F32)
         both = jnp.dot(row_x, w_in[...], preferred_element_type=F32)
+        arrive(source, 1)
+        row_dy = rows_dy[source].reshape(batch, width)
         back_act = jnp.dot(row_dy, w_down[...], preferred_element_type=F32)
         gate_pre = both[:, :hidden]
         up_part = both[:, hidden:]
@@ -188,18 +239,6 @@
             def _():
                 row_copy(source, seat).start()
 
-    below_count = layer
-    above_count = outer - 1 - layer
-    paired = jnp.minimum(below_count, above_count)
-
-    def turn(q):
-        odd = lax.rem(q, 2)
-        in_pairs = (q <= 2 * paired).astype(jnp.int32)
-        far = in_pairs * ((q + 1) // 2) + (1 - in_pairs) * (q - paired)
-        longer = (below_count > above_count).astype(jnp.int32)
-        from_below = in_pairs * odd + (1 - in_pairs) * longer
-        return layer + far - 2 * far * from_below, from_below
-
     for part in range(PIECES):
         @pl.when(layer < outer - 1)
         def _():
@@ -208,51 +247,77 @@
         @pl.when(layer > 0)
         def _():
             hop(layer, part, False, True).start()
-    pick(layer, tok_ref)
-    load_in.wait()
-    load_down.wait()
-    for swap in swaps:
-        swap.wait()
-
-    @pl.loop(0, width // 64)
-    def _(i):
-        at = pl.ds(pl.multiple_of(i * 64, 64), 64)
-        mine = mask_ref[0:1, :1].astype(BF16)
-        theirs = mask_ref[1:2, :1].astype(BF16)
-        w_in[at] = mine * w_in[at] + theirs * other_in[at]
-        w_down[at] = mine * w_down[at] + theirs * other_down[at]
+    pick(layer, x_ref, 0)
+    pick(layer, dy_ref, 1)
 
     @pl.loop(1, outer + 1)
-    def _(q):
-        @pl.when(q < outer)
+    def _(far):
+        below = layer - far
+        above = layer + far
+
+        @pl.when(far < outer)
         def _():
-            source, from_below = turn(q)
-            for part in range(PIECES):
-                hop(source, part, True, False).wait_recv()
-
-                @pl.when((from_below == 1) & (layer < outer - 1))
-                def _():
-                    hop(source, part, True, False).start()
-
-                @pl.when((from_below == 0) & (layer > 0))
-                def _():
-                    hop(source, part, False, False).start()
-            pick(source, held.at[source])
-
-        work(turn(q - 1)[0])
+            for kind, parts, box in ((0, (0, 1, 2), held_x), (1, (3, 4), held_dy)):
+                for part in parts:
+                    @pl.when(below >= 0)
+                    def _():
+                        hop(below, part, True, False).wait_recv()
+
+                        @pl.when(layer < outer - 1)
+                        def _():
+                            hop(below, part, True, False).start()
+
+                    @pl.when(above < outer)
+                    def _():
+                        hop(above, part, False, False).wait_recv()
+
+                        @pl.when(layer > 0)
+                        def _():
+                            hop(above, part, False, False).start()
+
+                @pl.loop(0, 2)
+                def _(way):
+                    source = layer + (2 * way - 1) * far
+
+                    @pl.when((source >= 0) & (source < outer))
+                    def _():
+                        pick(source, box.at[source], kind)
+
+        @pl.when(far == 1)
+        def _():
+            load_in.wait()
+            load_down.wait()
+            for swap in swaps:
+                swap.wait()
+
+            @pl.loop(0, width // 64)
+            def _(i):
+                at = pl.ds(pl.multiple_of(i * 64, 64), 64)
+                own = flags[0:1, :1].astype(BF16)
+                theirs = flags[1:2, :1].astype(BF16)
+                w_in[at] = own * w_in[at] + theirs * other_in[at]
+                w_down[at] = own * w_down[at] + theirs * other_down[at]
+
+        @pl.loop(0, 2)
+        def _(way):
+            source = layer + (2 * way - 1) * (far - 1)
+
+            @pl.when((source >= 0) & (source < outer) & (far + way > 1))
+            def _():
+                work(source)
 
     total = outer * batch
     grads = both_grads[...].reshape(total, 2 * hidden)
     acts = gated[...].reshape(total, hidden)
 
-    def part_of(group, begin, other):
-        columns = pl.ds(pl.multiple_of(begin + group * share, share), share)
-        some = rows[:, :, :, columns].reshape(total, share)
+    def part_of(group, box, other):
+        columns = pl.ds(pl.multiple_of(group * share, share), share)
+        some = box[:, :, :, columns].reshape(total, share)
         return lax.dot_general(some, other, (((0,), (0,)), ((), ())), preferred_element_type=F32)
 
     kinds = (
-        (0, grads, sib_in, from_in, cross_in, got_in, grad_in_ref),
-        (width, acts, sib_down, from_down, cross_down, got_down, grad_down_ref),
+        (rows_x, grads, sib_in, from_in, cross_in, got_in, grad_in_ref),
+        (rows_dy, acts, sib_down, from_down, cross_down, got_down, grad_down_ref),
     )
 
     def to_sibling(kind, which):
@@ -265,12 +330,12 @@
 
     for which, target in ((0, 1 - side), (1, side)):
         for kind in range(2):
-            begin, other, sib = kinds[kind][:3]
-            sib[which] = part_of(target * 2 + 1 - core, begin, other).astype(BF16)
+            box, other, sib = kinds[kind][:3]
+            sib[which] = part_of(target * 2 + 1 - core, box, other).astype(BF16)
             to_sibling(kind, which).start()
         for kind in range(2):
-            begin, other, _, arrived, crossing, _, out = kinds[kind]
-            mine = part_of(target * 2 + core, begin, other)
+            box, other, _, arrived, crossing, _, out = kinds[kind]
+            mine = part_of(target * 2 + core, box, other)
             to_sibling(kind, which).wait_recv()
             joined = (mine + arrived[which].astype(F32)).astype(BF16)
             if which == 0:
@@ -285,9 +350,9 @@
     def _(off):
         row_arrival(lax.rem(my_sender + off, senders)).wait_recv()
 
-    places = lax.broadcasted_iota(jnp.int32, (tok_count, senders * cap), 1)
-    first = (slots_ref[:, 0:1] == places).astype(F32)
-    second = (slots_ref[:, 1:2] == places).astype(F32)
+    places = lax.broadcasted_iota(jnp.int32, (tok_count, senders * cap), 1).astype(F32)
+    first = (marks[:, 0:1] == places).astype(F32)
+    second = (marks[:, 1:2] == places).astype(F32)
     chosen = (first + second).astype(BF16)
     for begin in range(0, width, 512):
         view = back[:, :, begin:begin + 512].reshape(senders * cap, 512)
@@ -311,15 +376,16 @@
             got, out = kinds[kind][5:]
             near = out[0, at].astype(F32)
             away = got[at].astype(F32)
-            lower = mask_ref[2:3, :1]
-            upper = mask_ref[3:4, :1]
+            lower = flags[2:3, :1]
+            upper = flags[3:4, :1]
             out[0, at] = (lower * near + upper * away).astype(BF16)
             out[1, at] = (upper * near + lower * away).astype(BF16)
 
     for source in range(outer):
         @pl.loop(1, plane)
         def _(off):
-            spread(source, off).wait_send()
+            spread(source, off, 0).wait_send()
+            spread(source, off, 1).wait_send()
 
         @pl.loop(0, plane)
         def _(seat):
@@ -487,61 +553,45 @@
     w_in = w_in_rep[0, 0]
     w_down = w_down_rep[0, 0]
     hidden = w_down.shape[1]
-    dest_rows = replica_of.reshape(-1)
-    row_ids = jnp.arange(tok_count * top_count, dtype=jnp.int32)
-    earlier = (dest_rows[:, None] == dest_rows[None, :]) & (row_ids[None, :] < row_ids[:, None])
-    rank_in = jnp.sum(earlier.astype(jnp.int32), axis=1).reshape(tok_count, top_count)
-    first_fits = (placement[2] != placement[0]) | (placement[3] != placement[0])
-    low_expert = jnp.where(first_fits, placement[0], placement[1])
-    side_table = jnp.where(placement == low_expert[None, :], 0, 1)
-    same = placement[:, None, :] == placement[None, :, :]
-    before = jnp.arange(groups)[None, :, None] < jnp.arange(groups)[:, None, None]
-    copy_table = jnp.sum((same & before).astype(jnp.int32), axis=1)
-    table = (side_table * groups + copy_table).reshape(-1)
-    named = replica_of[:, :, None] == jnp.arange(devices, dtype=jnp.int32)
-    entry = jnp.sum(jnp.where(named, table, 0), axis=2)
-    side_of = entry // groups
-    spot = entry % groups * cap + rank_in
-    cap = (groups - 1) * cap
-    lane_of = replica_of % lanes
-    seat_of = side_of * inner + lane_of % inner
-    facts = jnp.concatenate(
+    routes = jnp.concatenate(
         [
-            gate_weights,
-            (lane_of // inner).astype(BF16),
-            (seat_of * cap + spot).astype(BF16),
-            jnp.zeros((tok_count, 128 - 3 * top_count), BF16),
+            replica_of.astype(F32),
+            gate_weights.astype(F32),
+            jnp.zeros((tok_count, 128 - 2 * top_count), F32),
         ],
         axis=1,
     )
-    tok = jnp.concatenate([tokens_in, grad_out, facts], axis=1)
-    full = tok.shape[1]
+    copies = jnp.pad(
+        jnp.tile(placement, (1, groups)).astype(F32), ((0, 8 - groups), (0, 128 - devices))
+    )
+    rows_each = cap
+    cap = (groups - 1) * cap
+    full = width + 128
     any_spec = pl.BlockSpec(memory_space=pl.ANY)
     vmem_spec = pl.BlockSpec(memory_space=pltpu.VMEM)
     dma = pltpu.SemaphoreType.DMA
     share = width // groups
-    my_group = lax.axis_index("grp")
-    my_lane = lax.axis_index("ep")
-    side = my_group // 2
-    my_expert = jnp.where(side == 0, low_expert[my_lane], 1 - low_expert[my_lane])
-    own_fits = placement[my_group, my_lane] == my_expert
-    choices = jnp.stack([own_fits, ~own_fits, my_expert == 0, my_expert == 1]).astype(F32)
-    mask = jnp.broadcast_to(jnp.pad(choices, (0, 4))[:, None], (8, 128))
     batch = plane * cap
     d_tokens, gates, grad_in, grad_down = pl.pallas_call(
-        functools.partial(layer_kernel, groups, lanes, inner, cap),
+        functools.partial(layer_kernel, groups, lanes, inner, rows_each),
         out_shape=(
             jax.ShapeDtypeStruct((tok_count, width), BF16),
             jax.ShapeDtypeStruct((tok_count, 128), BF16),
             jax.ShapeDtypeStruct((KPC, share, 2 * hidden), BF16),
             jax.ShapeDtypeStruct((KPC, share, hidden), BF16),
         ),
-        in_specs=[vmem_spec, vmem_spec, vmem_spec, any_spec, any_spec],
+        in_specs=[vmem_spec] * 4 + [any_spec] * 2,
         out_specs=(vmem_spec,) * 4,
         scratch_shapes=[
-            pltpu.VMEM((outer, tok_count, full), BF16),
+            pltpu.VMEM((outer, tok_count, 128), BF16),
+            pltpu.VMEM((outer, tok_count, width), BF16),
+            pltpu.VMEM((outer, tok_count, width), BF16),
             pltpu.VMEM((outer, plane, cap, full), BF16),
+            pltpu.VMEM((outer, plane, cap, width), BF16),
             pltpu.VMEM((outer, plane, cap, full), BF16),
+            pltpu.VMEM((outer, plane, cap, width), BF16),
+            pltpu.VMEM((tok_count, 128), F32),
+            pltpu.VMEM((8, 128), F32),
             pltpu.VMEM((width, 2 * hidden), BF16),
             pltpu.VMEM((width, hidden), BF16),
             pltpu.VMEM((width, 2 * hidden), BF16),
@@ -561,9 +611,9 @@
             dma((outer, PIECES)),
             dma((outer, PIECES)),
             dma((outer, PIECES)),
-            dma((outer, plane)),
-            dma((outer, plane)),
-            dma((outer,)),
+            dma((2, outer, plane)),
+            dma((2, outer, plane)),
+            dma((2, outer)),
             dma((2,)),
             dma((outer, plane)),
             dma((senders,)),
@@ -579,7 +629,7 @@
             collective_id=0, has_side_effects=True, vmem_limit_bytes=58 * 2**20
         ),
         name="layer_backward",
-    )(tok, (side_of * lanes + lane_of) * cap + spot, mask, w_in, w_down)
+    )(tokens_in, grad_out, routes, copies, w_in, w_down)
     return d_tokens, gates[:, :top_count], grad_in, grad_down
 
 

time: 217 us -> 180 us (0.83)
  Pallas kernels: 193 us -> 166 us
  local copies, waits for them, and re-layouts: 15.1 us -> 9.02 us
  other arithmetic: 5.72 us -> 2.08 us
    pallas_call x1, Pallas kernels: 193 us -> 166 us  [shards(): pl.pallas_call(functools.partial(layer_kernel, groups, lanes, inner, rows...]
    concatenate x1, local copies, waits for them, and re-layouts: 3.05 us -> 0.07 us  [shards(): jnp.concatenate([replica_of.astype(F32), gate_weights.astype(F32), jnp.ze...]
    unnamed x8 -> x6, local copies, waits for them, and re-layouts: 8.94 us -> 7.37 us
where the time goes in v4:
time: 180 us; the launch traced here: 178 us
  Pallas kernels  166 us (92%)
  local copies, waits for them, and re-layouts  9.02 us (5%)
  other arithmetic  2.08 us (1%)
    pallas_call x1, Pallas kernels, shards(): pl.pallas_call(functools.partial(layer_kernel, groups, lanes, inner, rows...  166 us
    unnamed x6, local copies, waits for them, and re-layouts  7.37 us

profile of v4, /device:TPU:5, one launch (start us, length us, event | category | flops | bytes accessed | tf_op | source)
XLA Modules:
  0.0 177.6 jit_solution(7660285521587595407)
XLA Ops:
  0.6 0.1 pad.7.clone
  0.7 0.7 convert_element_type.15
  1.4 0.7 convert_element_type.17
  2.1 0.1 convert_element_type.18
  2.2 0.6 pad.4.copies_ref
  2.8 0.1 copy.11
  2.9 0.8 copy.12
  3.7 0.7 maximum_maximum_fusion.routes_ref
  4.4 165.9 %layer_backward.1 = (bf16[128,2048]{1,0:T(8,128)(2,1)}, bf16[128,128]{1,0:T(8,128)(2,1)}, bf16[2,512,1024]{2,1,0:T(8,128)(2,1)}, bf16[2,512,512]{2,1,0:T(8,128)(2,1)}) custom-call(bf16[128,2048]{1,0:T(8,128)(2,1)} %x_ref.1, bf16[128,2048]{1,0:T(8,128)(2,1)} %dy_ref.1, f32[128,128]{1,0:T(8,128)} %maximum_maximum_fusion.routes_ref, f32[8,128]{1,0:T(8,128)} %pad.4.copies_ref, ...), custom_call_target="tpu_custom_call" | custom-call | tf_op jit(solution)/shard_map/layer_backward/pallas_call | solution.py:575
  170.3 1.4 copy.13
  171.6 1.9 %copy.17 = bf16[128,2048]{1,0:T(8,128)(2,1)} copy(bf16[128,2048]{1,0:T(8,128)(2,1)} %get-tuple-element.20) | data formatting | bytes 1048576
  173.5 0.0 copy-start
  173.5 3.2 %copy.18 = bf16[2,512,1024]{2,1,0:T(8,128)(2,1)} copy(bf16[2,512,1024]{2,1,0:T(8,128)(2,1)} %get-tuple-element.22) | data formatting | bytes 4194304
  176.7 0.0 copy-done
  176.7 1.0 copy.19
  (2 shorter events, 0.0 us)
Async XLA Ops:
  173.5 3.2 %copy-start = (bf16[2,512,512]{2,1,0:T(8,128)(2,1)S(1)}, bf16[2,512,512]{2,1,0:T(8,128)(2,1)}, u32[]{:S(2)}) copy-start(bf16[2,512,512]{2,1,0:T(8,128)(2,1)} %get-tuple-element.23) | copy-start | bytes 3145732

commit v5 on v4

--- a/solution.py
+++ b/solution.py
@@ -17,13 +17,14 @@
 def layer_kernel(groups, lanes, inner, cap, x_ref, dy_ref, routes_ref, copies_ref,
                  w_in_hbm, w_down_hbm,
                  tokens_ref, gates_ref, grad_in_ref, grad_down_ref,
-                 held_facts, held_x, held_dy, picked_x, picked_dy, rows_x, rows_dy, marks, flags,
+                 held_facts, held_x, held_dy, picked_x, picked_dy, rows_x, rows_dy, marks, far_marks, flags,
+                 near_sums, far_sums, got_sums,
                  w_in, w_down, other_in, other_down,
                  both_grads, gated, row_grads, back,
                  sib_in, sib_down, from_in, from_down, cross_in, cross_down, got_in, got_down,
                  up_send, down_send, chain_recv, plane_send, plane_recv, own_sem, load_sem,
                  row_send, row_recv, row_own, swap_send, swap_recv, sib_send, sib_recv,
-                 cross_send, cross_recv):
+                 cross_send, cross_recv, side_send, side_recv):
     tok_count, width = x_ref.shape
     full = width + 128
     rows_each = cap
@@ -42,7 +43,7 @@
     side = my_group // 2
     core = lax.rem(my_group, 2)
     my_seat = side * inner + lax.rem(my_lane, inner)
-    my_sender = side * lanes + my_lane
+    my_within = lax.rem(my_lane, inner)
     sibling = (side * 2 + 1 - core, my_lane)
     across = ((1 - side) * 2 + core, my_lane)
     half = tok_count // 2
@@ -120,6 +121,8 @@
         backs = jnp.where(column_ids == k, look(back_table) + rank, backs)
     held_facts[layer] = facts.astype(BF16)
     marks[...] = backs
+    swap_marks = remote(marks, far_marks, side_send.at[0], side_recv.at[0], across)
+    swap_marks.start()
 
     def hop(source, part, upward, own):
         if part == 0:
@@ -148,26 +151,46 @@
             src.at[source, my_seat], dst.at[source, my_seat], own_sem.at[kind, source])
 
     def row_copy(source, seat):
-        return pltpu.make_async_remote_copy(
-            src_ref=row_grads.at[source, seat],
-            dst_ref=back.at[my_sender],
-            send_sem=row_send.at[source, seat],
-            recv_sem=row_recv.at[my_sender],
-            device_id=(seat // inner * 2 + core, source * inner + lax.rem(seat, inner)),
-            device_id_type=MESH,
-        )
-
-    def row_arrival(peer):
-        return pltpu.make_async_remote_copy(
-            src_ref=row_grads.at[0, 0],
-            dst_ref=back.at[peer],
-            send_sem=row_send.at[0, 0],
-            recv_sem=row_recv.at[peer],
-            device_id=(peer // lanes * 2 + core, lax.rem(peer, lanes)),
-            device_id_type=MESH,
-        )
-
-    row_stay = pltpu.make_async_copy(row_grads.at[layer, my_seat], back.at[my_sender], row_own)
+        slot = seat // inner * lanes + my_lane
+        return remote(row_grads.at[source, seat], back.at[slot], row_send.at[source, seat],
+                      row_recv.at[slot], (my_group, source * inner + lax.rem(seat, inner)))
+
+    def row_arrival(slot):
+        return remote(row_grads.at[0, 0], back.at[slot], row_send.at[0, 0], row_recv.at[slot],
+                      (my_group, lax.rem(slot, lanes)))
+
+    def row_stay(which):
+        return pltpu.make_async_copy(
+            row_grads.at[layer, which * inner + my_within],
+            back.at[which * lanes + my_lane], row_own.at[which])
+
+    def stays(source, seat):
+        return (source == layer) & (lax.rem(seat, inner) == my_within)
+
+    swap_sums = remote(far_sums, got_sums, side_send.at[1], side_recv.at[1], across)
+
+    def combine(which, places_of, out):
+        row_stay(which).wait()
+
+        @pl.loop(1, lanes)
+        def _(off):
+            row_arrival(which * lanes + lax.rem(my_lane + off, lanes)).wait_recv()
+
+        places = lax.broadcasted_iota(jnp.int32, (tok_count, lanes * cap), 1).astype(F32)
+        places = places + (side * lanes * cap).astype(F32)
+        first = (places_of[:, 0:1] == places).astype(F32)
+        second = (places_of[:, 1:2] == places).astype(F32)
+        chosen = (first + second).astype(BF16)
+        slots = pl.ds(which * lanes, lanes)
+        for begin in range(0, width, 512):
+            view = back[slots, :, begin:begin + 512].reshape(lanes * cap, 512)
+            out[:, begin:begin + 512] = jnp.dot(
+                chosen, view, preferred_element_type=F32).astype(BF16)
+        tail = back[slots, :, width:].reshape(lanes * cap, 128)
+        gate_first = jnp.dot(first.astype(BF16), tail, preferred_element_type=F32)
+        gate_second = jnp.dot(second.astype(BF16), tail, preferred_element_type=F32)
+        lane_ids = lax.broadcasted_iota(jnp.int32, (tok_count, 128), 1)
+        out[:, width:] = jnp.where(lane_ids == 0, gate_first, gate_second).astype(BF16)
 
     def pick(source, view, kind):
         facts = held_facts[source].astype(F32).T
@@ -229,11 +252,11 @@
 
         @pl.loop(0, plane)
         def _(seat):
-            mine = (source == layer) & (seat == my_seat)
+            mine = stays(source, seat)
 
             @pl.when(mine)
             def _():
-                row_stay.start()
+                row_stay(seat // inner).start()
 
             @pl.when(jnp.logical_not(mine))
             def _():
@@ -343,26 +366,18 @@
                 to_across(kind).start()
             else:
                 out[0] = joined
-
-    row_stay.wait()
-
-    @pl.loop(1, senders)
-    def _(off):
-        row_arrival(lax.rem(my_sender + off, senders)).wait_recv()
-
-    places = lax.broadcasted_iota(jnp.int32, (tok_count, senders * cap), 1).astype(F32)
-    first = (marks[:, 0:1] == places).astype(F32)
-    second = (marks[:, 1:2] == places).astype(F32)
-    chosen = (first + second).astype(BF16)
+        if which == 0:
+            swap_marks.wait()
+            combine(1 - side, far_marks, far_sums)
+            swap_sums.start()
+
+    combine(side, marks, near_sums)
+    swap_sums.wait()
     for begin in range(0, width, 512):
-        view = back[:, :, begin:begin + 512].reshape(senders * cap, 512)
-        tokens_ref[:, begin:begin + 512] = jnp.dot(
-            chosen, view, preferred_element_type=F32).astype(BF16)
-    tail = back[:, :, width:].reshape(senders * cap, 128)
-    gate_first = jnp.dot(first.astype(BF16), tail, preferred_element_type=F32)
-    gate_second = jnp.dot(second.astype(BF16), tail, preferred_element_type=F32)
-    lane_ids = lax.broadcasted_iota(jnp.int32, (tok_count, 128), 1)
-    gates_ref[...] = jnp.where(lane_ids == 0, gate_first, gate_second).astype(BF16)
+        at = slice(begin, begin + 512)
+        tokens_ref[:, at] = (near_sums[:, at].astype(F32) + got_sums[:, at].astype(F32)).astype(BF16)
+    gates_ref[...] = (
+        near_sums[:, width:].astype(F32) + got_sums[:, width:].astype(F32)).astype(BF16)
 
     for kind in range(2):
         to_across(kind).wait()
@@ -389,7 +404,7 @@
 
         @pl.loop(0, plane)
         def _(seat):
-            @pl.when(jnp.logical_not((source == layer) & (seat == my_seat)))
+            @pl.when(jnp.logical_not(stays(source, seat)))
             def _():
                 row_copy(source, seat).wait_send()
 
@@ -591,7 +606,11 @@
             pltpu.VMEM((outer, plane, cap, full), BF16),
             pltpu.VMEM((outer, plane, cap, width), BF16),
             pltpu.VMEM((tok_count, 128), F32),
+            pltpu.VMEM((tok_count, 128), F32),
             pltpu.VMEM((8, 128), F32),
+            pltpu.VMEM((tok_count, full), BF16),
+            pltpu.VMEM((tok_count, full), BF16),
+            pltpu.VMEM((tok_count, full), BF16),
             pltpu.VMEM((width, 2 * hidden), BF16),
             pltpu.VMEM((width, hidden), BF16),
             pltpu.VMEM((width, 2 * hidden), BF16),
@@ -617,11 +636,13 @@
             dma((2,)),
             dma((outer, plane)),
             dma((senders,)),
-            dma,
+            dma((2,)),
             dma((2,)),
             dma((2,)),
             dma((2, 2)),
             dma((2, 2)),
+            dma((2,)),
+            dma((2,)),
             dma((2,)),
             dma((2,)),
         ],

time: 180 us -> 188 us (1.044)
  the two profiles are of different devices: /device:TPU:5 before, /device:TPU:30 now
where the time goes in v5:
time: 188 us
  Pallas kernels  176 us (94%)
  local copies, waits for them, and re-layouts  9.02 us (5%)
  other arithmetic  2.08 us (1%)
    pallas_call x1, Pallas kernels, shards(): pl.pallas_call(functools.partial(layer_kernel, groups, lanes, inner, rows...  176 us
    unnamed x6, local copies, waits for them, and re-layouts  7.37 us

profile of v5, /device:TPU:30, one launch (start us, length us, event | category | flops | bytes accessed | tf_op | source)
XLA Modules:
  0.0 188.0 jit_solution(8958527613618137360)
XLA Ops:
  0.6 0.1 pad.7.clone
  0.7 0.7 convert_element_type.15
  1.4 0.7 convert_element_type.17
  2.1 0.1 convert_element_type.18
  2.2 0.6 pad.4.copies_ref
  2.8 0.1 copy.11
  2.9 0.8 copy.12
  3.7 0.7 maximum_maximum_fusion.routes_ref
  4.4 176.3 %layer_backward.1 = (bf16[128,2048]{1,0:T(8,128)(2,1)}, bf16[128,128]{1,0:T(8,128)(2,1)}, bf16[2,512,1024]{2,1,0:T(8,128)(2,1)}, bf16[2,512,512]{2,1,0:T(8,128)(2,1)}) custom-call(bf16[128,2048]{1,0:T(8,128)(2,1)} %x_ref.1, bf16[128,2048]{1,0:T(8,128)(2,1)} %dy_ref.1, f32[128,128]{1,0:T(8,128)} %maximum_maximum_fusion.routes_ref, f32[8,128]{1,0:T(8,128)} %pad.4.copies_ref, ...), custom_call_target="tpu_custom_call" | custom-call | tf_op jit(solution)/shard_map/layer_backward/pallas_call | solution.py:590
  180.6 1.4 copy.13
  182.0 1.9 copy.17
  183.9 0.0 copy-start
  183.9 3.2 %copy.18 = bf16[2,512,1024]{2,1,0:T(8,128)(2,1)} copy(bf16[2,512,1024]{2,1,0:T(8,128)(2,1)} %get-tuple-element.22) | data formatting | bytes 4194304
  187.0 0.0 copy-done
  187.0 1.0 copy.19
  (2 shorter events, 0.0 us)
Async XLA Ops:
  183.9 3.2 %copy-start = (bf16[2,512,512]{2,1,0:T(8,128)(2,1)S(1)}, bf16[2,512,512]{2,1,0:T(8,128)(2,1)}, u32[]{:S(2)}) copy-start(bf16[2,512,512]{2,1,0:T(8,128)(2,1)} %get-tuple-element.23) | copy-start | bytes 3145732

commit v6 on v4

--- a/solution.py
+++ b/solution.py
@@ -59,20 +59,6 @@
         peer = lax.rem(me + off, devices)
         pl.semaphore_signal(barrier, inc=1, device_id=(peer // lanes, lax.rem(peer, lanes)),
                             device_id_type=MESH)
-
-    pl.semaphore_wait(barrier, devices - 1)
-
-    def remote(src, dst, send, recv, device):
-        return pltpu.make_async_remote_copy(
-            src_ref=src, dst_ref=dst, send_sem=send, recv_sem=recv,
-            device_id=device, device_id_type=MESH)
-
-    swaps = [
-        remote(w_in_hbm, other_in, swap_send.at[0], swap_recv.at[0], sibling),
-        remote(w_down_hbm, other_down, swap_send.at[1], swap_recv.at[1], sibling),
-    ]
-    for swap in swaps:
-        swap.start()
 
     device_ids = lax.broadcasted_iota(jnp.int32, (1, 128), 1)
     group_ids = device_ids // lanes
@@ -121,6 +107,17 @@
     held_facts[layer] = facts.astype(BF16)
     marks[...] = backs
 
+    pl.semaphore_wait(barrier, devices - 1)
+
+    def remote(src, dst, send, recv, device):
+        return pltpu.make_async_remote_copy(
+            src_ref=src, dst_ref=dst, send_sem=send, recv_sem=recv,
+            device_id=device, device_id_type=MESH)
+
+    swaps = [
+        remote(w_in_hbm, other_in, swap_send.at[0], swap_recv.at[0], sibling),
+        remote(w_down_hbm, other_down, swap_send.at[1], swap_recv.at[1], sibling),
+    ]
     def hop(source, part, upward, own):
         if part == 0:
             src = dst = held_facts.at[source]
@@ -249,6 +246,8 @@
             hop(layer, part, False, True).start()
     pick(layer, x_ref, 0)
     pick(layer, dy_ref, 1)
+    for swap in swaps:
+        swap.start()
 
     @pl.loop(1, outer + 1)
     def _(far):

time: 180 us -> 180 us (level)
  no operation moved by 1% of the time
where the time goes in v6:
time: 180 us; the launch traced here: 177 us
  Pallas kernels  165 us (92%)
  local copies, waits for them, and re-layouts  9.02 us (5%)
  other arithmetic  2.08 us (1%)
    pallas_call x1, Pallas kernels, shards(): pl.pallas_call(functools.partial(layer_kernel, groups, lanes, inner, rows...  165 us
    unnamed x6, local copies, waits for them, and re-layouts  7.37 us

profile of v6, /device:TPU:5, one launch (start us, length us, event | category | flops | bytes accessed | tf_op | source)
XLA Modules:
  0.0 177.0 jit_solution(13025705603634633944)
XLA Ops:
  0.6 0.1 pad.7.clone
  0.7 0.7 convert_element_type.15
  1.4 0.7 convert_element_type.17
  2.1 0.1 convert_element_type.18
  2.2 0.6 pad.4.copies_ref
  2.8 0.1 copy.11
  2.9 0.8 copy.12
  3.7 0.7 maximum_maximum_fusion.routes_ref
  4.4 165.2 %layer_backward.1 = (bf16[128,2048]{1,0:T(8,128)(2,1)}, bf16[128,128]{1,0:T(8,128)(2,1)}, bf16[2,512,1024]{2,1,0:T(8,128)(2,1)}, bf16[2,512,512]{2,1,0:T(8,128)(2,1)}) custom-call(bf16[128,2048]{1,0:T(8,128)(2,1)} %x_ref.1, bf16[128,2048]{1,0:T(8,128)(2,1)} %dy_ref.1, f32[128,128]{1,0:T(8,128)} %maximum_maximum_fusion.routes_ref, f32[8,128]{1,0:T(8,128)} %pad.4.copies_ref, ...), custom_call_target="tpu_custom_call" | custom-call | tf_op jit(solution)/shard_map/layer_backward/pallas_call | solution.py:574
  169.6 1.4 copy.13
  171.0 1.9 %copy.17 = bf16[128,2048]{1,0:T(8,128)(2,1)} copy(bf16[128,2048]{1,0:T(8,128)(2,1)} %get-tuple-element.20) | data formatting | bytes 1048576
  172.9 0.0 copy-start
  172.9 3.2 %copy.18 = bf16[2,512,1024]{2,1,0:T(8,128)(2,1)} copy(bf16[2,512,1024]{2,1,0:T(8,128)(2,1)} %get-tuple-element.22) | data formatting | bytes 4194304
  176.0 0.0 copy-done
  176.0 1.0 copy.19
  (2 shorter events, 0.0 us)
Async XLA Ops:
  172.9 3.2 %copy-start = (bf16[2,512,512]{2,1,0:T(8,128)(2,1)S(1)}, bf16[2,512,512]{2,1,0:T(8,128)(2,1)}, u32[]{:S(2)}) copy-start(bf16[2,512,512]{2,1,0:T(8,128)(2,1)} %get-tuple-element.23) | copy-start | bytes 3145732
